TPU v7x, 256 devices: a whole 4x4x8 slice. The times are simulated.
256 devices in a mesh: row: 16 (over z_lo, y, core), col: 16 (over z_hi, x).
Axes of the slice: x: 4, y: 4, z: 8 (z_hi: 4, z_lo: 2; z = z_hi * 2 + z_lo), core: 2. Of those that a mesh axis runs over, the one named last changes fastest.
Arguments:
- states_now: float32 [40, 32768], P(None, ('col', 'row')), may hold values from -60 to 60
- states_next: float32 [40, 32768], P(None, ('row', 'col')), may hold values from -60 to 60
- states_last: float32 [40, 32768], P(None, ('col', 'row')), may hold values from -60 to 60
- payoff_now: bfloat16 [64, 32768], P(None, ('col', 'row')), may hold values from 0 to 2
- payoff_next: bfloat16 [64, 32768], P(None, ('row', 'col')), may hold values from 0 to 2
- payoff_last: bfloat16 [64, 32768], P(None, ('col', 'row')), may hold values from 0 to 2
Outputs:
- value_next: float32 [64, 32768], P(None, ('row', 'col'))
- value_now: float32 [64, 32768], P(None, ('col', 'row'))
All inputs are finite; a program needn't handle non-finite values.
Results may differ from a plain program's by a relative error of at most 0.0003.
Values sent between devices are 32-bit elements; how exact they have to be, the bound alone decides.
A program may use at most 128 MiB of HBM per device.

v0:
```python
import math

import jax
import jax.numpy as jnp
from jax import lax
from jax.sharding import PartitionSpec as P


def log_kernel(row_states, col_states, row_norms, col_norms):
    cross_term = lax.dot_general(
        row_states,
        col_states,
        (((0,), (0,)), ((), ())),
        precision=lax.Precision.HIGHEST,
        preferred_element_type=jnp.float32,
    )
    return cross_term - 0.5 * row_norms[:, None] - 0.5 * col_norms[None, :]


def log_blocks(row_states, col_states):
    factors, points = row_states.shape
    block_rows = math.gcd(points, 512)
    block_count = points // block_rows
    blocks = row_states.reshape(factors, block_count, block_rows).transpose(1, 0, 2)
    norms = jnp.sum(row_states * row_states, axis=0).reshape(block_count, block_rows)
    col_norms = jnp.sum(col_states * col_states, axis=0)

    def build(block_item):
        row_piece, piece_norms = block_item
        return log_kernel(row_piece, col_states, piece_norms, col_norms)

    return lax.map(build, (blocks, norms))


def local_stats(log_weight):
    col_peak = jnp.max(log_weight, axis=(0, 1))
    col_sum = jnp.sum(jnp.exp(log_weight - col_peak[None, None, :]), axis=(0, 1))
    return (col_peak, col_sum)


def stats_row(col_peak, col_sum):
    global_peak = lax.pmax(col_peak, "row")
    global_sum = lax.psum(col_sum * jnp.exp(col_peak - global_peak), "row")
    return (global_peak, global_sum)


def continuation(log_weight, later_value, col_peak, col_sum):
    scaled = (later_value / col_sum[None, :]).astype(jnp.bfloat16)

    def project(weight_block):
        kernel = jnp.exp(weight_block - col_peak[None, :]).astype(jnp.bfloat16)
        return lax.dot_general(
            scaled, kernel, (((1,), (1,)), ((), ())), preferred_element_type=jnp.float32
        )

    pieces = lax.map(project, log_weight)
    block_count, block_rows = (log_weight.shape[0], log_weight.shape[1])
    return pieces.transpose(1, 0, 2).reshape(scaled.shape[0], block_count * block_rows)


def per_device(states_now, states_next, states_last, payoff_now, payoff_next, payoff_last):
    later_states, later_values = (
        lax.all_gather(states_last, "row", axis=1, tiled=True),
        lax.all_gather(payoff_last.astype(jnp.float32), "row", axis=1, tiled=True),
    )
    next_rows = lax.all_gather(states_next, "col", axis=1, tiled=True)
    weights = log_blocks(next_rows, later_states)
    col_peak, col_sum = local_stats(weights)
    col_peak, col_sum = stats_row(col_peak, col_sum)
    partial_value = continuation(weights, later_values, col_peak, col_sum)
    own_next = lax.psum_scatter(partial_value, "col", scatter_dimension=1, tiled=True)
    value_next = jnp.maximum(payoff_next.astype(jnp.float32), own_next)
    now_rows = lax.all_gather(states_now, "col", axis=1, tiled=True)
    next_cols, value_cols = (
        lax.all_gather(states_next, "row", axis=1, tiled=True),
        lax.all_gather(value_next, "row", axis=1, tiled=True),
    )
    weights = log_blocks(now_rows, next_cols)
    col_peak, col_sum = local_stats(weights)
    col_peak, col_sum = stats_row(col_peak, col_sum)
    partial_value = continuation(weights, value_cols, col_peak, col_sum)
    own_block = lax.psum_scatter(partial_value, "col", scatter_dimension=1, tiled=True)
    value_now = jnp.maximum(payoff_now.astype(jnp.float32), own_block)
    return (value_next, value_now)


def solution(mesh):
    in_specs = (
        P(None, ("col", "row")),
        P(None, ("row", "col")),
        P(None, ("col", "row")),
        P(None, ("col", "row")),
        P(None, ("row", "col")),
        P(None, ("col", "row")),
    )
    out_specs = (P(None, ("row", "col")), P(None, ("col", "row")))
    return jax.shard_map(
        per_device, mesh=mesh, in_specs=in_specs, out_specs=out_specs, check_vma=False
    )
```

profile of v0, /device:TPU:1, one launch (start us, length us, event | category | flops | bytes accessed | tf_op | source)
XLA Modules:
  0.0 562.3 jit_solution(17174039601657234633)
XLA Ops:
  7.2 42.6 %all_gather.21 = f32[40,2048]{1,0:T(8,128)S(1)} all-gather(f32[40,128]{1,0:T(8,128)} %param.14), channel_id=1, replica_groups=mesh['row'=16,'col'=16] {'col'}, dimensions={1}, use_global_device_ids=true | all-gather | bytes 348160 | tf_op jit(solution)/shard_map/all_gather | solution.py:73
  50.1 27.8 %all_gather.22 = f32[40,2048]{1,0:T(8,128)S(1)} all-gather(f32[40,128]{1,0:T(8,128)} %param.15), channel_id=1, replica_groups=mesh['row'=16,'col'=16] {'row'}, dimensions={1}, use_global_device_ids=true | all-gather | bytes 348160 | tf_op jit(solution)/shard_map/all_gather | solution.py:75
  77.9 33.9 %all_gather.18 = f32[40,2048]{1,0:T(8,128)S(1)} all-gather(f32[40,128]{1,0:T(8,128)} %param.15), channel_id=1, replica_groups=mesh['row'=16,'col'=16] {'col'}, dimensions={1}, use_global_device_ids=true | all-gather | bytes 348160 | tf_op jit(solution)/shard_map/all_gather | solution.py:66
  112.1 7.8 %broadcast.49.clone.1 = f32[4,512,2048]{2,1,0:T(8,128)} broadcast(f32[]{:T(128)} %constant.47.clone.1), dimensions={} | broadcast | bytes 16777220 | tf_op jit(solution)/shard_map/broadcast.11
  120.0 21.0 %while.42 = (s32[]{:T(128)}, f32[4,512,2048]{2,1,0:T(8,128)}, f32[4,40,512]{2,0,1:T(4,128)S(1)}, f32[40,2048]{1,0:T(8,128)S(1)}, f32[4,512]{1,0:T(4,128)S(1)}, /*index=5*/f32[2048]{0:T(1024)S(1)}, s32[]{:T(128)}) while((s32[]{:T(128)}, f32[4,512,2048]{2,1,0:T(8,128)}, f32[4,40,512]{2,0,1:T(4,128)S(1)}, f32[40,2048]{1,0:T(8,128)S(1)}, ...), condition=%wide.region_14.15_spmd, body=%wide.region_13.14_spmd.sunk | while | flops 505416192 | bytes 4799061 | solution.py:32
  120.1 5.2 bitcast_dynamic-update-slice_fusion.5
  130.6 5.2 bitcast_dynamic-update-slice_fusion.5
  141.0 22.9 %all_gather.19 = f32[40,2048]{1,0:T(8,128)S(1)} all-gather(f32[40,128]{1,0:T(8,128)S(1)} %copy-done.1), channel_id=1, replica_groups=mesh['row'=16,'col'=16] {'row'}, dimensions={1}, use_global_device_ids=true | all-gather | bytes 348160 | tf_op jit(solution)/shard_map/all_gather | solution.py:63
  164.0 7.8 %broadcast.49.clone = f32[4,512,2048]{2,1,0:T(8,128)} broadcast(f32[]{:T(128)} %constant.47.clone.1), dimensions={} | broadcast | bytes 16777220 | tf_op jit(solution)/shard_map/broadcast.11
  171.8 21.0 %while.40 = (s32[]{:T(128)}, f32[4,512,2048]{2,1,0:T(8,128)}, f32[4,40,512]{2,0,1:T(4,128)S(1)}, f32[40,2048]{1,0:T(8,128)S(1)}, f32[4,512]{1,0:T(4,128)S(1)}, /*index=5*/f32[2048]{0:T(1024)S(1)}, s32[]{:T(128)}) while((s32[]{:T(128)}, f32[4,512,2048]{2,1,0:T(8,128)}, f32[4,40,512]{2,0,1:T(4,128)S(1)}, f32[40,2048]{1,0:T(8,128)S(1)}, ...), condition=%wide.region_3.4_spmd, body=%wide.region_2.3_spmd.sunk | while | flops 505416192 | bytes 4799061 | solution.py:32
  171.9 5.2 bitcast_dynamic-update-slice_fusion.4
  182.4 5.2 bitcast_dynamic-update-slice_fusion.4
  192.8 6.6 %reduce_max.19 = f32[2048]{0:T(1024)S(1)} reduce(f32[4,512,2048]{2,1,0:T(8,128)} %get-tuple-element.384, f32[]{:T(128)} %constant.48.clone.1), dimensions={0,1}, to_apply=%region_15.16 | reduce | flops 4192256 | bytes 16785412 | tf_op jit(solution)/shard_map/reduce_max | solution.py:36
  199.4 6.6 %reduce_max.18 = f32[2048]{0:T(1024)S(1)} reduce(f32[4,512,2048]{2,1,0:T(8,128)} %get-tuple-element.366, f32[]{:T(128)} %constant.48.clone.1), dimensions={0,1}, to_apply=%region_4.5 | reduce | flops 4192256 | bytes 16785412 | tf_op jit(solution)/shard_map/reduce_max | solution.py:36
  206.0 8.1 %exponential_reduce_fusion = f32[2048]{0:T(1024)S(1)} fusion(f32[4,512,2048]{2,1,0:T(8,128)} %get-tuple-element.384, f32[2048]{0:T(1024)S(1)} %reduce_max.19), kind=kLoop, calls=%fused_computation.24 | loop fusion | flops 8386560 | bytes 16793600 | tf_op jit(solution)/shard_map/reduce_sum | solution.py:37
  214.1 50.4 %all-reduce.1 = (f32[2048]{0:T(1024)S(1)}, f32[2048]{0:T(1024)S(1)}) all-reduce(f32[2048]{0:T(1024)S(1)} %reduce_max.18, f32[2048]{0:T(1024)S(1)} %reduce_max.19), channel_id=1, replica_groups=mesh['row'=16,'col'=16] {'row'}, use_global_device_ids=true, to_apply=%region_5.6 | all-reduce | flops 4096 | bytes 32768 | tf_op jit(solution)/shard_map/pmax | solution.py:42
  264.5 8.1 %exponential_reduce_fusion.1 = f32[2048]{0:T(1024)S(1)} fusion(f32[4,512,2048]{2,1,0:T(8,128)} %get-tuple-element.366, f32[2048]{0:T(1024)S(1)} %reduce_max.18), kind=kLoop, calls=%fused_computation.25 | loop fusion | flops 8386560 | bytes 16793600 | tf_op jit(solution)/shard_map/reduce_sum | solution.py:37
  272.6 21.8 %all_gather.20 = f32[64,2048]{1,0:T(8,128)S(1)} all-gather(f32[64,128]{1,0:T(8,128)S(1)} %convert_element_type.22), channel_id=1, replica_groups=mesh['row'=16,'col'=16] {'row'}, dimensions={1}, use_global_device_ids=true | all-gather | bytes 557056 | tf_op jit(solution)/shard_map/all_gather | solution.py:64
  294.4 50.3 %all-reduce = (f32[2048]{0:T(1024)S(1)}, f32[2048]{0:T(1024)S(1)}) all-reduce(f32[2048]{0:T(1024)S(1)} %get-tuple-element.185, f32[2048]{0:T(1024)S(1)} %get-tuple-element.184), channel_id=1, replica_groups=mesh['row'=16,'col'=16] {'row'}, use_global_device_ids=true, to_apply=%region_7.8 | all-reduce | flops 4096 | bytes 32768 | tf_op jit(solution)/shard_map/psum | solution.py:43
  344.8 11.9 %while.41 = (s32[]{:T(128)}, f32[4,64,512]{2,1,0:T(8,128)S(1)}, f32[4,512,2048]{2,1,0:T(8,128)}, f32[2048]{0:T(1024)S(1)}, bf16[64,2048]{1,0:T(8,128)(2,1)S(1)}, /*index=5*/s32[]{:T(128)}) while((s32[]{:T(128)}, f32[4,64,512]{2,1,0:T(8,128)S(1)}, f32[4,512,2048]{2,1,0:T(8,128)}, f32[2048]{0:T(1024)S(1)}, bf16[64,2048]{1,0:T(8,128)(2,1)S(1)}, ...), condition=%wide.region_9.10_spmd, body=%wide.region_8.9_spmd.sunk | while | flops 136314880 | bytes 4596805 | solution.py:56
  357.6 81.5 %reduce-scatter.3.cloned.1.call-done = f32[64,128]{1,0:T(8,128)} async-done(((f32[64,2048]{1,0:T(8,128)}), f32[64,128]{1,0:T(8,128)}) %reduce-scatter.3.cloned.1.call-update) | async-done | bytes 32784 | tf_op jit(solution)/shard_map/reduce_scatter | solution.py:71
  439.9 22.6 %all_gather.23 = f32[64,2048]{1,0:T(8,128)S(1)} all-gather(f32[64,128]{1,0:T(8,128)S(1)} %convert_maximum_fusion.1), channel_id=1, replica_groups=mesh['row'=16,'col'=16] {'row'}, dimensions={1}, use_global_device_ids=true | all-gather | bytes 557056 | tf_op jit(solution)/shard_map/all_gather | solution.py:76
  462.5 11.9 %while.43 = (s32[]{:T(128)}, f32[4,64,512]{2,1,0:T(8,128)S(1)}, f32[4,512,2048]{2,1,0:T(8,128)}, f32[2048]{0:T(1024)S(1)}, bf16[64,2048]{1,0:T(8,128)(2,1)S(1)}, /*index=5*/s32[]{:T(128)}) while((s32[]{:T(128)}, f32[4,64,512]{2,1,0:T(8,128)S(1)}, f32[4,512,2048]{2,1,0:T(8,128)}, f32[2048]{0:T(1024)S(1)}, bf16[64,2048]{1,0:T(8,128)(2,1)S(1)}, ...), condition=%wide.region_20.21_spmd, body=%wide.region_19.20_spmd.sunk | while | flops 136314880 | bytes 4596805 | solution.py:56
  475.3 78.7 %reduce-scatter.5.cloned.1.call-done = f32[64,128]{1,0:T(8,128)} async-done(((f32[64,2048]{1,0:T(8,128)}), f32[64,128]{1,0:T(8,128)}) %reduce-scatter.5.cloned.1.call-update) | async-done | bytes 32784 | tf_op jit(solution)/shard_map/reduce_scatter | solution.py:82
  (68 shorter events, 49.6 us)
Async XLA Ops:
  7.2 431.9 %reduce-scatter.3.cloned.1.call-start = ((), (), s32[]{:S(2)}) async-start(), calls=%async_computation.2 | async-start | bytes 557056 | tf_op jit(solution)/shard_map/reduce_scatter | solution.py:71
  112.1 28.9 %copy-start.1 = (f32[40,128]{1,0:T(8,128)S(1)}, f32[40,128]{1,0:T(8,128)}, u32[]{:S(2)}) copy-start(f32[40,128]{1,0:T(8,128)} %param.16) | copy-start | bytes 61444
  206.0 66.6 %copy-start.2 = (bf16[64,128]{1,0:T(8,128)(2,1)S(1)}, bf16[64,128]{1,0:T(8,128)(2,1)}, u32[]{:S(2)}) copy-start(bf16[64,128]{1,0:T(8,128)(2,1)} %param.19) | copy-start | bytes 49156
  272.6 166.5 %copy-start.3 = (bf16[64,128]{1,0:T(8,128)(2,1)S(1)}, bf16[64,128]{1,0:T(8,128)(2,1)}, u32[]{:S(2)}) copy-start(bf16[64,128]{1,0:T(8,128)(2,1)} %param.18) | copy-start | bytes 49156
  356.7 197.3 %copy-start.4 = (bf16[64,128]{1,0:T(8,128)(2,1)S(1)}, bf16[64,128]{1,0:T(8,128)(2,1)}, u32[]{:S(2)}) copy-start(bf16[64,128]{1,0:T(8,128)(2,1)} %param.17) | copy-start | bytes 49156
  357.6 196.5 %reduce-scatter.5.cloned.1.call-start = ((), (), s32[]{:S(2)}) async-start(), calls=%async_computation.3 | async-start | bytes 557056 | tf_op jit(solution)/shard_map/reduce_scatter | solution.py:82
  439.8 115.6 %copy-start = (f32[64,128]{1,0:T(8,128)}, f32[64,128]{1,0:T(8,128)S(1)}, u32[]{:S(2)}) copy-start(f32[64,128]{1,0:T(8,128)S(1)} %convert_maximum_fusion.1) | copy-start | bytes 98308
Sparse Core Ops, SparseCore 0:
  357.7 81.3 reduce-scatter.2
  475.4 78.5 reduce-scatter.4
where the time goes:
time: 564 us; the launch traced here: 562 us
  blocking collectives  272 us (48%)
  waiting for transfers between devices  160 us (28%)
  matrix products  64.8 us (11%)
  other arithmetic  31.9 us (6%)
  local copies, waits for them, and re-layouts  18.5 us (3%)
  between operations  14.2 us (3%)
    reduce_scatter x2, waiting for transfers between devices, per_device(): lax.psum_scatter(partial_value, 'col', scatter_dimension=1, tiled=True)  160 us
    pmax x1, blocking collectives, stats_row(): global_peak = lax.pmax(col_peak, 'row')  50.4 us
    psum x1, blocking collectives, stats_row(): global_sum = lax.psum(col_sum * jnp.exp(col_peak - global_peak), 'row')  50.3 us
    all_gather x1, blocking collectives, per_device(): now_rows = lax.all_gather(states_now, 'col', axis=1, tiled=True)  42.6 us
    dot_general x8, matrix products, log_kernel(): lax.dot_general(row_states, col_states, (((0,), (0,)), ((), ())), precisi...  41.2 us
    all_gather x1, blocking collectives, per_device(): next_rows = lax.all_gather(states_next, 'col', axis=1, tiled=True)  33.9 us
    all_gather x1, blocking collectives, per_device(): lax.all_gather(states_next, 'row', axis=1, tiled=True)  27.8 us
    dot_general x8, matrix products, project(): lax.dot_general(scaled, kernel, (((1,), (1,)), ((), ())), preferred_eleme...  23.7 us
  transfers between devices with their start and end apart: 2, of which 2 were waited for; matrix products, arithmetic and copies ran while one was open for 0% of the time, Pallas kernels for 0%

commit v1 on v0

v1 whole, which is shorter than its diff:
```python
import jax
import jax.numpy as jnp
from jax import lax
from jax.experimental import pallas as pl
from jax.experimental.pallas import tpu as pltpu
from jax.sharding import PartitionSpec as P

F32, BF16 = jnp.float32, jnp.bfloat16
W = 128
SIDE = 16
QUAD = 4
HALF = 8
MESH = pl.DeviceIdType.MESH


def span(block, width):
    return pl.ds(pl.multiple_of(block * width, width), width)


def loop(count, body):
    def step(k, carry):
        body(k)
        return carry

    lax.fori_loop(0, count, step, 0)


def split3(v):
    high = v.astype(BF16).astype(F32)
    rest = v - high
    mid = rest.astype(BF16).astype(F32)
    return high, mid, rest - mid


def operand(block, earlier):
    high, mid, low = split3(block)
    norm = split3(-0.5 * jnp.sum(block * block, axis=0, keepdims=True))
    row = lax.broadcasted_iota(jnp.int32, (8, block.shape[1]), 0)
    extra = jnp.where(row < 6, 1.0, 0.0)
    for k in range(3):
        extra = jnp.where(row == (k if earlier else k + 3), norm[k], extra)
    pieces = (high, high, mid, mid, high, low) if earlier else (high, mid, high, mid, low, high)
    return jnp.concatenate(pieces + (extra, jnp.zeros_like(extra)), axis=0)


def build_later(states, later):
    def one(k):
        later[:, span(k, W)] = operand(states[k], False).astype(BF16)

    loop(SIDE, one)


def build_earlier(states, earlier):
    def one(k):
        earlier[span(k, W), :] = operand(states[k], True).T.astype(BF16)

    loop(SIDE, one)


def log_pass(earlier, later, log_kernel, peak):
    rows, cols = 256, 256

    def col(jc):
        js = span(jc, cols)

        def row(ic, top):
            i = span(ic, rows)
            tile = jnp.dot(earlier[i, :], later[:, js], preferred_element_type=F32)
            log_kernel[i, js] = tile
            return jnp.maximum(top, jnp.max(tile.reshape(rows // 8, 8, cols), axis=0))

        count = log_kernel.shape[0] // rows
        top = lax.fori_loop(0, count, row, jnp.full((8, cols), -jnp.inf, F32), unroll=True)
        peak[:, js] = jnp.max(top, axis=0, keepdims=True)

    loop(log_kernel.shape[1] // cols, col)


def exp_pass(log_kernel, kernel, peak, density):
    rows, cols = 64, 256

    def col(jc):
        js = span(jc, cols)
        top = jnp.broadcast_to(peak[:, js], (8, cols))

        def row(ic, total):
            i = span(ic, rows)
            tile = jnp.exp(log_kernel[i, js].reshape(rows // 8, 8, cols) - top[None])
            kernel[i, js] = tile.reshape(rows, cols).astype(BF16)
            return total + jnp.sum(tile, axis=0)

        count = log_kernel.shape[0] // rows
        total = lax.fori_loop(0, count, row, jnp.zeros((8, cols), F32), unroll=4)
        density[:, js] = jnp.sum(total, axis=0, keepdims=True)

    loop(log_kernel.shape[1] // cols, col)


def remote(src, dst, send, recv, row, col):
    return pltpu.make_async_remote_copy(
        src_ref=src, dst_ref=dst, send_sem=send, recv_sem=recv, device_id=(row, col), device_id_type=MESH
    )


def wait_for(ref, sem):
    pltpu.make_async_copy(ref, ref, sem).wait()


class Place:
    def __init__(self):
        self.row, self.col = lax.axis_index("row"), lax.axis_index("col")
        self.chip, self.core = self.row // 2, self.row % 2
        self.z, self.x = self.col // QUAD, self.col % QUAD
        self.twin = self.chip * 2 + 1 - self.core

    def on_core(self, k):
        return ((self.chip + k) % HALF) * 2 + self.core

    def along_z(self, k):
        return ((self.z + k) % QUAD) * QUAD + self.x

    def along_x(self, k):
        return self.z * QUAD + (self.x + k) % QUAD


def row_send(me, own, buf, send, recv):
    def one(k):
        remote(own, buf.at[me.row], send, recv.at[me.row], me.on_core(k + 1), me.col).start()

    loop(HALF - 1, one)
    remote(own, buf.at[me.row], send, recv.at[me.row], me.twin, me.col).start()


def row_relay(me, buf, send, recv):
    def one(k):
        slot = me.on_core(HALF - 1 - k)
        wait_for(buf.at[slot], recv.at[slot])
        remote(buf.at[slot], buf.at[slot], send, recv.at[slot], me.twin, me.col).start()

    loop(HALF - 1, one)


def row_finish(me, buf, recv):
    def one(k):
        slot = k * 2 + 1 - me.core
        wait_for(buf.at[slot], recv.at[slot])

    loop(HALF, one)


def col_send(me, own, buf, send, recv):
    def one(k):
        remote(own, buf.at[me.col], send, recv.at[me.col], me.row, me.along_z(k + 1)).start()

    loop(QUAD - 1, one)

    def two(k):
        remote(own, buf.at[me.col], send, recv.at[me.col], me.row, me.along_x(k + 1)).start()

    loop(QUAD - 1, two)


def col_relay(me, buf, send, recv):
    def one(k):
        slot = me.along_z(QUAD - 1 - k)
        wait_for(buf.at[slot], recv.at[slot])

        def two(q):
            remote(buf.at[slot], buf.at[slot], send, recv.at[slot], me.row, me.along_x(q + 1)).start()

        loop(QUAD - 1, two)

    loop(QUAD - 1, one)


def col_finish(me, buf, recv):
    def one(k):
        def two(q):
            slot = k * QUAD + (me.x + q + 1) % QUAD
            wait_for(buf.at[slot], recv.at[slot])

        loop(QUAD - 1, two)

    loop(QUAD, one)


def stat_send(me, buf, send, recv):
    own = buf.at[me.row]

    def one(k):
        remote(own, own, send, recv, (me.row + k + 1) % SIDE, me.col).start()

    loop(SIDE - 1, one)


def stat_finish(buf, recv, out, combine):
    wait_for(buf.at[pl.ds(0, SIDE - 1)], recv)
    total = buf[0]
    for k in range(1, SIDE):
        total = combine(total, buf[k])
    out[...] = total


def product_send(me, scaled, kernel, part, arrived, send, recv):
    def zs(k):
        z = (me.z + k + 1) % QUAD

        def xs(q):
            x = (me.x + q + 1) % QUAD
            slot = z * QUAD + x
            rows = kernel[span(slot, W), :]
            part[slot] = lax.dot_general(
                scaled[...], rows, (((1,), (1,)), ((), ())), preferred_element_type=F32
            )
            return x, slot

        def away(q):
            x, slot = xs(q)
            remote(part.at[slot], arrived.at[z, me.x], send, recv.at[z], me.row, me.z * QUAD + x).start()

        loop(QUAD - 1, away)
        x, slot = xs(QUAD - 1)
        arrived[z, me.x] = part[slot]

    loop(QUAD, zs)


def sum_send(me, arrived, sums, final, send, recv_x, recv_z):
    def one(k):
        z = (me.z + k + 1) % QUAD
        wait_for(arrived.at[z, pl.ds(0, QUAD - 1)], recv_x.at[z])
        sums[z] = arrived[z, 0] + arrived[z, 1] + arrived[z, 2] + arrived[z, 3]
        remote(sums.at[z], final.at[me.z], send, recv_z, me.row, z * QUAD + me.x).start()

    loop(QUAD - 1, one)
    wait_for(arrived.at[me.z, pl.ds(0, QUAD - 1)], recv_x.at[me.z])
    final[me.z] = arrived[me.z, 0] + arrived[me.z, 1] + arrived[me.z, 2] + arrived[me.z, 3]


def sum_finish(final, recv_z):
    wait_for(final.at[pl.ds(0, QUAD - 1)], recv_z)
    return final[0] + final[1] + final[2] + final[3]


def kernel_body(
    now_ref, next_ref, last_ref, pay_now, pay_next, pay_last, out_next, out_now,
    x1, y1, x2, y2, v1, v2, own_v,
    earlier1, later1, earlier2, later2, log1, log2, kern, scaled,
    peaks1, dens1, peaks2, dens2, peak, density1, density2, stat_row,
    part1, arrived1, sums1, final1, part2, arrived2, sums2, final2,
    own_sem, gather_send, stat_send_sem, sum_send_x, sum_send_z,
    recv_gather, recv_stat, recv_x, recv_z,
):
    me = Place()

    barrier = pltpu.get_barrier_semaphore()

    def greet_row(k):
        pl.semaphore_signal(barrier, inc=1, device_id=((me.row + k + 1) % SIDE, me.col), device_id_type=MESH)

    loop(SIDE - 1, greet_row)

    def greet_col(k):
        pl.semaphore_signal(barrier, inc=1, device_id=(me.row, me.along_z(k + 1)), device_id_type=MESH)
        pl.semaphore_signal(barrier, inc=1, device_id=(me.row, me.along_x(k + 1)), device_id_type=MESH)

    loop(QUAD - 1, greet_col)

    own = [
        pltpu.make_async_copy(next_ref, x1.at[me.col], own_sem.at[0]),
        pltpu.make_async_copy(last_ref, y1.at[me.row], own_sem.at[1]),
        pltpu.make_async_copy(now_ref, x2.at[me.col], own_sem.at[2]),
        pltpu.make_async_copy(next_ref, y2.at[me.row], own_sem.at[3]),
    ]
    for copy in own:
        copy.start()
    own_v[0] = pay_last[...].astype(F32)
    v1[me.row] = own_v[0]
    for copy in own:
        copy.wait()
    pl.semaphore_wait(barrier, SIDE - 1 + 2 * (QUAD - 1))

    g = lambda k: (gather_send.at[k], recv_gather.at[k])
    col_send(me, next_ref, x1, *g(0))
    row_send(me, last_ref, y1, *g(1))
    col_relay(me, x1, *g(0))
    row_relay(me, y1, *g(1))
    col_send(me, now_ref, x2, *g(2))
    row_send(me, next_ref, y2, *g(3))
    row_send(me, own_v.at[0], v1, *g(4))
    row_finish(me, y1, recv_gather.at[1])
    build_later(y1, later1)
    col_finish(me, x1, recv_gather.at[0])
    build_earlier(x1, earlier1)

    log_pass(earlier1, later1, log1, stat_row)
    peaks1[me.row] = stat_row[...]
    stat_send(me, peaks1, stat_send_sem.at[0], recv_stat.at[0])

    col_relay(me, x2, *g(2))
    row_relay(me, y2, *g(3))
    row_relay(me, v1, *g(4))

    stat_finish(peaks1, recv_stat.at[0], peak, jnp.maximum)
    exp_pass(log1, kern, peak, stat_row)
    dens1[me.row] = stat_row[...]
    stat_send(me, dens1, stat_send_sem.at[1], recv_stat.at[1])

    row_finish(me, y2, recv_gather.at[3])
    build_later(y2, later2)
    col_finish(me, x2, recv_gather.at[2])
    build_earlier(x2, earlier2)
    row_finish(me, v1, recv_gather.at[4])

    stat_finish(dens1, recv_stat.at[1], density1, jnp.add)

    def scale(values, density):
        def one(k):
            js = span(k, W)
            scaled[:, js] = (values[k] / density[:, js]).astype(BF16)

        loop(SIDE, one)

    scale(v1, density1)
    product_send(me, scaled, kern, part1, arrived1, sum_send_x.at[0], recv_x.at[0])

    log_pass(earlier2, later2, log2, stat_row)
    peaks2[me.row] = stat_row[...]
    stat_send(me, peaks2, stat_send_sem.at[2], recv_stat.at[2])
    sum_send(me, arrived1, sums1, final1, sum_send_z.at[0], recv_x.at[0], recv_z.at[0])
    value_next = jnp.maximum(pay_next[...].astype(F32), sum_finish(final1, recv_z.at[0]))
    out_next[...] = value_next
    own_v[1] = value_next
    v2[me.row] = value_next
    row_send(me, own_v.at[1], v2, *g(5))

    stat_finish(peaks2, recv_stat.at[2], peak, jnp.maximum)
    exp_pass(log2, kern, peak, stat_row)
    dens2[me.row] = stat_row[...]
    stat_send(me, dens2, stat_send_sem.at[3], recv_stat.at[3])
    row_relay(me, v2, *g(5))
    row_finish(me, v2, recv_gather.at[5])
    stat_finish(dens2, recv_stat.at[3], density2, jnp.add)
    scale(v2, density2)
    product_send(me, scaled, kern, part2, arrived2, sum_send_x.at[1], recv_x.at[1])
    sum_send(me, arrived2, sums2, final2, sum_send_z.at[1], recv_x.at[1], recv_z.at[1])
    out_now[...] = jnp.maximum(pay_now[...].astype(F32), sum_finish(final2, recv_z.at[1]))

    for k, buf in ((0, x1), (1, y1), (2, x2), (3, y2), (4, v1), (5, v2)):
        wait_for(buf.at[pl.ds(0, SIDE - 1)], gather_send.at[k])
    for k, buf in ((0, peaks1), (1, dens1), (2, peaks2), (3, dens2)):
        wait_for(buf.at[pl.ds(0, SIDE - 1)], stat_send_sem.at[k])
    for k, part, final in ((0, part1, final1), (1, part2, final2)):
        wait_for(part.at[pl.ds(0, QUAD * (QUAD - 1))], sum_send_x.at[k])
        wait_for(final.at[pl.ds(0, QUAD - 1)], sum_send_z.at[k])


def per_device(states_now, states_next, states_last, payoff_now, payoff_next, payoff_last):
    factors, width = states_now.shape
    swaps = payoff_now.shape[0]
    points = SIDE * width
    states = pltpu.VMEM((SIDE, factors, width), F32)
    values = pltpu.VMEM((SIDE, swaps, width), F32)
    stats = pltpu.VMEM((SIDE, 1, points), F32)
    line = pltpu.VMEM((1, points), F32)
    quad = pltpu.VMEM((QUAD, swaps, width), F32)
    square = pltpu.VMEM((QUAD, QUAD, swaps, width), F32)
    sums = [values, square, quad, quad]
    dma = pltpu.SemaphoreType.DMA
    vmem = pl.BlockSpec(memory_space=pltpu.VMEM)
    out = jax.ShapeDtypeStruct((swaps, width), F32)
    return pl.pallas_call(
        kernel_body,
        out_shape=(out, out),
        in_specs=[vmem] * 6,
        out_specs=(vmem, vmem),
        scratch_shapes=[states] * 4
        + [values, values, pltpu.VMEM((2, swaps, width), F32)]
        + [pltpu.VMEM((points, 256), BF16), pltpu.VMEM((256, points), BF16)] * 2
        + [pltpu.VMEM((points, points), F32)] * 2
        + [pltpu.VMEM((points, points), BF16), pltpu.VMEM((swaps, points), BF16)]
        + [stats] * 4
        + [line] * 4
        + sums * 2
        + [dma((4,)), dma((6,)), dma((4,)), dma((2,)), dma((2,))]
        + [dma((6, SIDE)), dma((4,)), dma((2, QUAD)), dma((2,))],
        compiler_params=pltpu.CompilerParams(
            collective_id=0, has_side_effects=True, vmem_limit_bytes=60 * 2**20
        ),
    )(states_now, states_next, states_last, payoff_now, payoff_next, payoff_last)


def solution(mesh):
    early, late = P(None, ("row", "col")), P(None, ("col", "row"))
    return jax.shard_map(
        per_device,
        mesh=mesh,
        in_specs=(late, early, late, late, early, late),
        out_specs=(early, late),
        check_vma=False,
    )
```

time: 564 us -> 78.2 us (0.14)
  blocking collectives: 272 us -> 0 us
  waiting for transfers between devices: 160 us -> 0 us
  Pallas kernels: 0 us -> 75.1 us
  matrix products: 64.8 us -> 0 us
  other arithmetic: 31.9 us -> 0 us
  local copies, waits for them, and re-layouts: 18.5 us -> 2 us
  between operations: 14.2 us -> 0.65 us
    all_gather x6 -> x0, blocking collectives: 172 us -> none  [the longest x1 42.6 us: per_device(): now_rows = lax.all_gather(states_now, 'col', axis=1, tiled=True)]
    reduce_scatter x2 -> x0, waiting for transfers between devices: 160 us -> none  [per_device(): lax.psum_scatter(partial_value, 'col', scatter_dimension=1, tiled=True)]
    pallas_call x0 -> x1, Pallas kernels: none -> 75.1 us  [per_device(): pl.pallas_call(kernel_body, out_shape=(out, out), in_specs=[vmem] * 6, ou...]
    dot_general x16 -> x0, matrix products: 64.8 us -> none  [the longest x8 41.2 us: log_kernel(): lax.dot_general(row_states, col_states, (((0,), (0,)), ((), ())), precisi...]
    pmax x1 -> x0, blocking collectives: 50.4 us -> none  [stats_row(): global_peak = lax.pmax(col_peak, 'row')]
    psum x1 -> x0, blocking collectives: 50.3 us -> none  [stats_row(): global_sum = lax.psum(col_sum * jnp.exp(col_peak - global_peak), 'row')]
    reduce_sum x6 -> x0, other arithmetic: 16.3 us -> none  [the longest x2 16.2 us: local_stats(): jnp.sum(jnp.exp(log_weight - col_peak[None, None, :]), axis=(0, 1))]
    another operation x4 -> x0, local copies, waits for them, and re-layouts: 15.8 us -> none
  transfers between devices with their start and end apart: 2 -> 0, of which waited for: 2 -> 0; matrix products, arithmetic and copies ran while one was open for 0% -> 0% of each run, Pallas kernels for 0% -> 0%
where the time goes in v1:
time: 78.2 us; the launch traced here: 77.7 us
  Pallas kernels  75.1 us (96%)
  local copies, waits for them, and re-layouts  2 us (3%)
    pallas_call x1, Pallas kernels, per_device(): pl.pallas_call(kernel_body, out_shape=(out, out), in_specs=[vmem] * 6, ou...  75.1 us
    unnamed x4, local copies, waits for them, and re-layouts  2 us

profile of v1, /device:TPU:1, one launch (start us, length us, event | category | flops | bytes accessed | tf_op | source)
XLA Modules:
  0.0 77.7 jit_solution(2065066974781942826)
XLA Ops:
  0.6 75.1 %shard_map.77 = (f32[64,128]{1,0:T(8,128)}, f32[64,128]{1,0:T(8,128)}) custom-call(f32[40,128]{1,0:T(8,128)} %now_ref.1, f32[40,128]{1,0:T(8,128)} %next_ref.1, f32[40,128]{1,0:T(8,128)} %last_ref.1, bf16[64,128]{1,0:T(8,128)(2,1)} %pay_now.1, bf16[64,128]{1,0:T(8,128)(2,1)} %pay_next.1, bf16[64,128]{1,0:T(8,128)(2,1)} %pay_last.1), custom_call_target="tpu_custom_call" | custom-call | tf_op jit(solution)/shard_map/pallas_call | solution.py:372
  75.7 0.0 copy-start
  75.7 1.4 %copy.10 = f32[64,128]{1,0:T(8,128)} copy(f32[64,128]{1,0:T(8,128)} %get-tuple-element.4) | data formatting | bytes 65536
  77.1 0.0 copy-done
  77.1 0.6 copy.11
Async XLA Ops:
  75.7 1.4 %copy-start = (f32[64,128]{1,0:T(8,128)S(1)}, f32[64,128]{1,0:T(8,128)}, u32[]{:S(2)}) copy-start(f32[64,128]{1,0:T(8,128)} %get-tuple-element.5) | copy-start | bytes 98308

commit v2 on v1

v2 whole, which is shorter than its diff:
```python
import jax
import jax.numpy as jnp
from jax import lax
from jax.experimental import pallas as pl
from jax.experimental.pallas import tpu as pltpu
from jax.sharding import PartitionSpec as P

F32, BF16 = jnp.float32, jnp.bfloat16
W = 128
SIDE = 16
QUAD = 4
HALVES = 2
HALF = 8
MESH = pl.DeviceIdType.MESH


def span(block, width):
    return pl.ds(pl.multiple_of(block * width, width), width)


def loop(count, body):
    def step(k, carry):
        body(k)
        return carry

    lax.fori_loop(0, count, step, 0)


def split3(v):
    high = v.astype(BF16).astype(F32)
    rest = v - high
    mid = rest.astype(BF16).astype(F32)
    return high, mid, rest - mid


def operand(block, earlier):
    high, mid, low = split3(block)
    norm = split3(-0.5 * jnp.sum(block * block, axis=0, keepdims=True))
    row = lax.broadcasted_iota(jnp.int32, (8, block.shape[1]), 0)
    extra = jnp.where(row < 6, 1.0, 0.0)
    for k in range(3):
        extra = jnp.where(row == (k if earlier else k + 3), norm[k], extra)
    pieces = (high, high, mid, mid, high, low) if earlier else (high, mid, high, mid, low, high)
    return jnp.concatenate(pieces + (extra, jnp.zeros_like(extra)), axis=0)


def build_later(states, later, k):
    later[:, span(k, W)] = operand(states[k], False).astype(BF16)


def build_earlier(states, earlier, k):
    earlier[span(k, W), :] = operand(states[k], True).T.astype(BF16)


def log_pass(earlier, later, log_kernel, stat, half):
    rows, cols = 256, 256
    blocks = log_kernel.shape[1] // cols // HALVES

    def col(jc):
        js = span(half * blocks + jc, cols)

        def row(ic, top):
            i = span(ic, rows)
            tile = jnp.dot(earlier[i, :], later[:, js], preferred_element_type=F32)
            log_kernel[i, js] = tile
            return jnp.maximum(top, jnp.max(tile.reshape(rows // 8, 8, cols), axis=0))

        count = log_kernel.shape[0] // rows
        top = lax.fori_loop(0, count, row, jnp.full((8, cols), -jnp.inf, F32), unroll=True)
        stat[:, span(jc, cols)] = jnp.max(top, axis=0, keepdims=True)

    loop(blocks, col)


def exp_pass(log_kernel, kernel, peak, stat, half):
    rows, cols = 64, 256
    blocks = log_kernel.shape[1] // cols // HALVES

    def col(jc):
        js = span(half * blocks + jc, cols)
        top = jnp.broadcast_to(peak[half, :, span(jc, cols)], (8, cols))

        def row(ic, total):
            i = span(ic, rows)
            tile = jnp.exp(log_kernel[i, js].reshape(rows // 8, 8, cols) - top[None])
            kernel[i, js] = tile.reshape(rows, cols).astype(BF16)
            return total + jnp.sum(tile, axis=0)

        count = log_kernel.shape[0] // rows
        total = lax.fori_loop(0, count, row, jnp.zeros((8, cols), F32), unroll=4)
        stat[:, span(jc, cols)] = jnp.sum(total, axis=0, keepdims=True)

    loop(blocks, col)


def scale(values, density, scaled):
    blocks = SIDE // HALVES

    def one(k):
        below = density[k // blocks, :, span(k % blocks, W)]
        scaled[:, span(k, W)] = (values[k] / below).astype(BF16)

    loop(SIDE, one)


def remote(src, dst, send, recv, row, col):
    return pltpu.make_async_remote_copy(
        src_ref=src, dst_ref=dst, send_sem=send, recv_sem=recv, device_id=(row, col), device_id_type=MESH
    )


def wait_for(ref, sem):
    pltpu.make_async_copy(ref, ref, sem).wait()


class Place:
    def __init__(self):
        self.row, self.col = lax.axis_index("row"), lax.axis_index("col")
        self.chip, self.core = self.row // 2, self.row % 2
        self.z, self.x = self.col // QUAD, self.col % QUAD
        self.twin = self.chip * 2 + 1 - self.core

    def on_core(self, k):
        return ((self.chip + k) % HALF) * 2 + self.core

    def along_z(self, k):
        return ((self.z + k) % QUAD) * QUAD + self.x

    def along_x(self, k):
        return self.z * QUAD + (self.x + k) % QUAD


def row_send(me, own, buf, send, recv):
    def one(k):
        remote(own, buf.at[me.row], send, recv.at[me.row], me.on_core(k + 1), me.col).start()

    loop(HALF - 1, one)
    remote(own, buf.at[me.row], send, recv.at[me.row], me.twin, me.col).start()


def row_relay(me, buf, send, recv, then=None):
    def one(k):
        slot = me.on_core(HALF - 1 - k)
        wait_for(buf.at[slot], recv.at[slot])
        remote(buf.at[slot], buf.at[slot], send, recv.at[slot], me.twin, me.col).start()
        if then:
            then(slot)

    loop(HALF - 1, one)


def row_finish(me, buf, recv, then=None):
    def one(k):
        slot = ((me.chip + HALF - k) % HALF) * 2 + 1 - me.core
        wait_for(buf.at[slot], recv.at[slot])
        if then:
            then(slot)

    loop(HALF, one)


def col_send(me, own, buf, send, recv):
    def one(k):
        remote(own, buf.at[me.col], send, recv.at[me.col], me.row, me.along_z(k + 1)).start()

    loop(QUAD - 1, one)

    def two(k):
        remote(own, buf.at[me.col], send, recv.at[me.col], me.row, me.along_x(k + 1)).start()

    loop(QUAD - 1, two)


def col_relay(me, buf, send, recv, then=None):
    def one(k):
        slot = me.along_z(QUAD - 1 - k)
        wait_for(buf.at[slot], recv.at[slot])

        def two(q):
            remote(buf.at[slot], buf.at[slot], send, recv.at[slot], me.row, me.along_x(q + 1)).start()

        loop(QUAD - 1, two)
        if then:
            then(slot)

    loop(QUAD - 1, one)


def col_finish(me, buf, recv, then=None):
    def one(k):
        def two(q):
            slot = ((me.z + QUAD - k) % QUAD) * QUAD + (me.x + q + 1) % QUAD
            wait_for(buf.at[slot], recv.at[slot])
            if then:
                then(slot)

        loop(QUAD - 1, two)

    loop(QUAD, one)


def stat_send(me, stat, buf, send, recv):
    buf[me.row] = stat[...]
    own = buf.at[me.row]

    def one(k):
        remote(own, own, send, recv, (me.row + k + 1) % SIDE, me.col).start()

    loop(SIDE - 1, one)


def stat_finish(buf, recv, out, half, combine):
    wait_for(buf.at[pl.ds(0, SIDE - 1)], recv)
    total = buf[0]
    for k in range(1, SIDE):
        total = combine(total, buf[k])
    out[half] = total


def product_send(me, scaled, kernel, part, arrived, send, recv):
    def zs(k):
        z = (me.z + k + 1) % QUAD
        rows = kernel[span(z, QUAD * W), :]
        product = lax.dot_general(scaled[...], rows, (((1,), (1,)), ((), ())), preferred_element_type=F32)
        for x in range(QUAD):
            part[z, x] = product[:, x * W : (x + 1) * W]

        def away(q):
            x = (me.x + q + 1) % QUAD
            remote(part.at[z, x], arrived.at[z, me.x], send, recv.at[z], me.row, me.z * QUAD + x).start()

        loop(QUAD - 1, away)
        arrived[z, me.x] = part[z, me.x]

    loop(QUAD, zs)


def sum_send(me, arrived, sums, final, send, recv_x, recv_z, first, count):
    def one(k):
        z = (me.z + first + k + 1) % QUAD
        wait_for(arrived.at[z, pl.ds(0, QUAD - 1)], recv_x.at[z])
        sums[z] = arrived[z, 0] + arrived[z, 1] + arrived[z, 2] + arrived[z, 3]
        remote(sums.at[z], final.at[me.z], send, recv_z, me.row, z * QUAD + me.x).start()

    loop(count, one)


def sum_own(me, arrived, final, recv_x):
    wait_for(arrived.at[me.z, pl.ds(0, QUAD - 1)], recv_x.at[me.z])
    final[me.z] = arrived[me.z, 0] + arrived[me.z, 1] + arrived[me.z, 2] + arrived[me.z, 3]


def sum_finish(final, recv_z):
    wait_for(final.at[pl.ds(0, QUAD - 1)], recv_z)
    return final[0] + final[1] + final[2] + final[3]


def kernel_body(
    now_ref, next_ref, last_ref, pay_next_ref, pay_last_ref, out_next, out_now,
    x1, y1, x2, y2, v1, v2, own_v, pay_next, pay_last,
    earlier1, later1, earlier2, later2, log1, log2, kern, scaled,
    peaks1, dens1, peaks2, dens2, peak, density1, density2, stat,
    part1, arrived1, sums1, final1, part2, arrived2, sums2, final2,
    own_sem, gather_send, stat_sent, sum_sent_x, sum_sent_z,
    recv_gather, recv_stat, recv_x, recv_z,
):
    me = Place()

    barrier = pltpu.get_barrier_semaphore()

    def greet_col(k):
        pl.semaphore_signal(barrier, inc=1, device_id=(me.row, me.along_z(k + 1)), device_id_type=MESH)
        pl.semaphore_signal(barrier, inc=1, device_id=(me.row, me.along_x(k + 1)), device_id_type=MESH)

    loop(QUAD - 1, greet_col)

    def greet_row(k):
        pl.semaphore_signal(barrier, inc=1, device_id=((me.row + k + 1) % SIDE, me.col), device_id_type=MESH)

    loop(SIDE - 1, greet_row)

    own = [
        pltpu.make_async_copy(src, dst, own_sem.at[k])
        for k, (src, dst) in enumerate(
            (
                (next_ref, x1.at[me.col]),
                (last_ref, y1.at[me.row]),
                (now_ref, x2.at[me.col]),
                (next_ref, y2.at[me.row]),
                (pay_next_ref, pay_next),
                (pay_last_ref, pay_last),
            )
        )
    ]
    for copy in own:
        copy.start()
    for copy in own:
        copy.wait()
    own_v[0] = pay_last[...].astype(F32)
    v1[me.row] = own_v[0]
    build_earlier(x1, earlier1, me.col)
    build_later(y1, later1, me.row)
    build_earlier(x2, earlier2, me.col)
    build_later(y2, later2, me.row)
    pl.semaphore_wait(barrier, SIDE - 1 + 2 * (QUAD - 1))

    g = lambda k: (gather_send.at[k], recv_gather.at[k])
    add_x1 = lambda k: build_earlier(x1, earlier1, k)
    add_y1 = lambda k: build_later(y1, later1, k)
    add_x2 = lambda k: build_earlier(x2, earlier2, k)
    add_y2 = lambda k: build_later(y2, later2, k)

    col_send(me, x1.at[me.col], x1, *g(0))
    row_send(me, y1.at[me.row], y1, *g(1))
    row_relay(me, y1, *g(1), add_y1)
    col_relay(me, x1, *g(0), add_x1)
    row_send(me, own_v.at[0], v1, *g(4))
    row_send(me, y2.at[me.row], y2, *g(3))
    col_send(me, x2.at[me.col], x2, *g(2))
    row_finish(me, y1, recv_gather.at[1], add_y1)
    col_finish(me, x1, recv_gather.at[0], add_x1)

    log_pass(earlier1, later1, log1, stat.at[0], 0)
    stat_send(me, stat.at[0], peaks1.at[0], stat_sent.at[0, 0], recv_stat.at[0, 0])
    row_relay(me, v1, *g(4))
    row_relay(me, y2, *g(3), add_y2)
    log_pass(earlier1, later1, log1, stat.at[0], 1)
    stat_send(me, stat.at[0], peaks1.at[1], stat_sent.at[0, 1], recv_stat.at[0, 1])
    col_relay(me, x2, *g(2), add_x2)
    row_finish(me, y2, recv_gather.at[3], add_y2)

    for half in range(HALVES):
        stat_finish(peaks1.at[half], recv_stat.at[0, half], peak, half, jnp.maximum)
        exp_pass(log1, kern, peak, stat.at[0], half)
        stat_send(me, stat.at[0], dens1.at[half], stat_sent.at[1, half], recv_stat.at[1, half])

    col_finish(me, x2, recv_gather.at[2], add_x2)
    row_finish(me, v1, recv_gather.at[4])
    for half in range(HALVES):
        log_pass(earlier2, later2, log2, stat.at[0], half)
        stat_send(me, stat.at[0], peaks2.at[half], stat_sent.at[2, half], recv_stat.at[2, half])

    for half in range(HALVES):
        stat_finish(dens1.at[half], recv_stat.at[1, half], density1, half, jnp.add)
    scale(v1, density1, scaled)
    product_send(me, scaled, kern, part1, arrived1, sum_sent_x.at[0], recv_x.at[0])

    sums = (arrived1, sums1, final1, sum_sent_z.at[0], recv_x.at[0], recv_z.at[0])
    for half in range(HALVES):
        stat_finish(peaks2.at[half], recv_stat.at[2, half], peak, half, jnp.maximum)
        exp_pass(log2, kern, peak, stat.at[0], half)
        stat_send(me, stat.at[0], dens2.at[half], stat_sent.at[3, half], recv_stat.at[3, half])
        if half == 0:
            sum_send(me, *sums, 0, QUAD - 1)
    sum_own(me, arrived1, final1, recv_x.at[0])
    held = sum_finish(final1, recv_z.at[0])
    out_next[...] = held
    value_next = jnp.maximum(pay_next[...].astype(F32), held)
    own_v[1] = value_next
    v2[me.row] = value_next
    row_send(me, own_v.at[1], v2, *g(5))

    for half in range(HALVES):
        stat_finish(dens2.at[half], recv_stat.at[3, half], density2, half, jnp.add)
    row_relay(me, v2, *g(5))
    row_finish(me, v2, recv_gather.at[5])
    scale(v2, density2, scaled)
    product_send(me, scaled, kern, part2, arrived2, sum_sent_x.at[1], recv_x.at[1])
    sum_send(me, arrived2, sums2, final2, sum_sent_z.at[1], recv_x.at[1], recv_z.at[1], 0, QUAD - 1)
    sum_own(me, arrived2, final2, recv_x.at[1])
    out_now[...] = sum_finish(final2, recv_z.at[1])

    for k, buf in ((0, x1), (1, y1), (2, x2), (3, y2), (4, v1), (5, v2)):
        wait_for(buf.at[pl.ds(0, SIDE - 1)], gather_send.at[k])
    for k, buf in ((0, peaks1), (1, dens1), (2, peaks2), (3, dens2)):
        for half in range(HALVES):
            wait_for(buf.at[half, pl.ds(0, SIDE - 1)], stat_sent.at[k, half])
    for k, part, final in ((0, part1, final1), (1, part2, final2)):
        wait_for(part.at[pl.ds(0, QUAD - 1)], sum_sent_x.at[k])
        wait_for(final.at[pl.ds(0, QUAD - 1)], sum_sent_z.at[k])


def per_device(states_now, states_next, states_last, payoff_now, payoff_next, payoff_last):
    factors, width = states_now.shape
    swaps = payoff_now.shape[0]
    points = SIDE * width
    states = pltpu.VMEM((SIDE, factors, width), F32)
    values = pltpu.VMEM((SIDE, swaps, width), F32)
    stats = pltpu.VMEM((HALVES, SIDE, 1, points // HALVES), F32)
    line = pltpu.VMEM((HALVES, 1, points // HALVES), F32)
    quad = pltpu.VMEM((QUAD, swaps, width), F32)
    square = pltpu.VMEM((QUAD, QUAD, swaps, width), F32)
    payoff = pltpu.VMEM((swaps, width), BF16)
    dma = pltpu.SemaphoreType.DMA
    vmem = pl.BlockSpec(memory_space=pltpu.VMEM)
    out = jax.ShapeDtypeStruct((swaps, width), F32)
    held_next, held_now = pl.pallas_call(
        kernel_body,
        out_shape=(out, out),
        in_specs=[pl.BlockSpec(memory_space=pl.ANY)] * 5,
        out_specs=(vmem, vmem),
        scratch_shapes=[states] * 4
        + [values, values, pltpu.VMEM((2, swaps, width), F32), payoff, payoff]
        + [pltpu.VMEM((points, 256), BF16), pltpu.VMEM((256, points), BF16)] * 2
        + [pltpu.VMEM((points, points), F32)] * 2
        + [pltpu.VMEM((points, points), BF16), pltpu.VMEM((swaps, points), BF16)]
        + [stats] * 4
        + [line] * 4
        + [square, square, quad, quad] * 2
        + [dma((6,)), dma((6,)), dma((4, HALVES)), dma((2,)), dma((2,))]
        + [dma((6, SIDE)), dma((4, HALVES)), dma((2, QUAD)), dma((2,))],
        compiler_params=pltpu.CompilerParams(
            collective_id=0, has_side_effects=True, vmem_limit_bytes=60 * 2**20
        ),
    )(states_now, states_next, states_last, payoff_next, payoff_last)
    return jnp.maximum(payoff_next.astype(F32), held_next), jnp.maximum(payoff_now.astype(F32), held_now)


def solution(mesh):
    early, late = P(None, ("row", "col")), P(None, ("col", "row"))
    return jax.shard_map(
        per_device,
        mesh=mesh,
        in_specs=(late, early, late, late, early, late),
        out_specs=(early, late),
        check_vma=False,
    )
```

time: 78.2 us -> 73.3 us (0.937)
  Pallas kernels: 75.1 us -> 71 us
  local copies, waits for them, and re-layouts: 2 us -> 0.01 us
  other arithmetic: 0 us -> 1.41 us
    pallas_call x1, Pallas kernels: 75.1 us -> 71 us  [per_device(): pl.pallas_call(kernel_body, out_shape=(out, out), in_specs=[pl.BlockSpec(...]
    unnamed x4, local copies, waits for them, and re-layouts: 2 us -> 0.01 us
    max x0 -> x1, other arithmetic: none -> 1.41 us  [per_device(): jnp.maximum(payoff_now.astype(F32), held_now)]
where the time goes in v2:
time: 73.3 us; the launch traced here: 73.1 us
  Pallas kernels  71 us (97%)
  other arithmetic  1.41 us (2%)
    pallas_call x1, Pallas kernels, per_device(): pl.pallas_call(kernel_body, out_shape=(out, out), in_specs=[pl.BlockSpec(...  71 us

profile of v2, /device:TPU:1, one launch (start us, length us, event | category | flops | bytes accessed | tf_op | source)
XLA Modules:
  0.0 73.1 jit_solution(14421692714927165414)
XLA Ops:
  0.6 0.0 copy-start
  0.6 0.0 copy-start.1
  0.7 71.0 %shard_map.77 = (f32[64,128]{1,0:T(8,128)}, f32[64,128]{1,0:T(8,128)}) custom-call(f32[40,128]{1,0:T(8,128)} %now_ref.1, f32[40,128]{1,0:T(8,128)} %next_ref.1, f32[40,128]{1,0:T(8,128)} %last_ref.1, bf16[64,128]{1,0:T(8,128)(2,1)} %pay_next_ref.1, bf16[64,128]{1,0:T(8,128)(2,1)} %pay_last_ref.1), custom_call_target="tpu_custom_call" | custom-call | tf_op jit(solution)/shard_map/pallas_call | solution.py:397
  71.7 0.0 copy-done
  71.7 0.0 copy-done.1
  71.7 1.4 %convert_maximum_fusion = (f32[64,128]{1,0:T(8,128)}, f32[64,128]{1,0:T(8,128)}) fusion(f32[64,128]{1,0:T(8,128)} %get-tuple-element.5, bf16[64,128]{1,0:T(8,128)(2,1)S(1)} %copy-done.1, f32[64,128]{1,0:T(8,128)} %get-tuple-element.4, bf16[64,128]{1,0:T(8,128)(2,1)S(1)} %copy-done), kind=kLoop, calls=%fused_computation | loop fusion | flops 32768 | bytes 163840 | tf_op jit(solution)/shard_map/max | solution.py:416
Async XLA Ops:
  0.6 71.1 %copy-start = (bf16[64,128]{1,0:T(8,128)(2,1)S(1)}, bf16[64,128]{1,0:T(8,128)(2,1)}, u32[]{:S(2)}) copy-start(bf16[64,128]{1,0:T(8,128)(2,1)} %pay_next_ref.1) | copy-start | bytes 49156
  0.6 71.1 %copy-start.1 = (bf16[64,128]{1,0:T(8,128)(2,1)S(1)}, bf16[64,128]{1,0:T(8,128)(2,1)}, u32[]{:S(2)}) copy-start(bf16[64,128]{1,0:T(8,128)(2,1)} %param.9) | copy-start | bytes 49156

commit v3 on v2

--- a/solution.py
+++ b/solution.py
@@ -52,24 +52,17 @@
     earlier[span(k, W), :] = operand(states[k], True).T.astype(BF16)
 
 
-def log_pass(earlier, later, log_kernel, stat, half):
-    rows, cols = 256, 256
-    blocks = log_kernel.shape[1] // cols // HALVES
-
-    def col(jc):
-        js = span(half * blocks + jc, cols)
-
-        def row(ic, top):
-            i = span(ic, rows)
+def log_tiles(earlier, later, log_kernel, top, first_row, rows, first_col, cols):
+    tile_rows, tile_cols = 256, 256
+    for jc in range(cols // tile_cols):
+        js = pl.ds(pl.multiple_of(first_col + jc * tile_cols, tile_cols), tile_cols)
+        highest = top[:, js]
+        for ic in range(rows // tile_rows):
+            i = pl.ds(pl.multiple_of(first_row + ic * tile_rows, tile_rows), tile_rows)
             tile = jnp.dot(earlier[i, :], later[:, js], preferred_element_type=F32)
             log_kernel[i, js] = tile
-            return jnp.maximum(top, jnp.max(tile.reshape(rows // 8, 8, cols), axis=0))
-
-        count = log_kernel.shape[0] // rows
-        top = lax.fori_loop(0, count, row, jnp.full((8, cols), -jnp.inf, F32), unroll=True)
-        stat[:, span(jc, cols)] = jnp.max(top, axis=0, keepdims=True)
-
-    loop(blocks, col)
+            highest = jnp.maximum(highest, jnp.max(tile.reshape(tile_rows // 8, 8, tile_cols), axis=0))
+        top[:, js] = highest
 
 
 def exp_pass(log_kernel, kernel, peak, stat, half):
@@ -87,7 +80,7 @@
             return total + jnp.sum(tile, axis=0)
 
         count = log_kernel.shape[0] // rows
-        total = lax.fori_loop(0, count, row, jnp.zeros((8, cols), F32), unroll=4)
+        total = lax.fori_loop(0, count, row, jnp.zeros((8, cols), F32), unroll=True)
         stat[:, span(jc, cols)] = jnp.sum(total, axis=0, keepdims=True)
 
     loop(blocks, col)
@@ -117,11 +110,13 @@
     def __init__(self):
         self.row, self.col = lax.axis_index("row"), lax.axis_index("col")
         self.chip, self.core = self.row // 2, self.row % 2
+        self.low, self.y = self.chip // QUAD, self.chip % QUAD
         self.z, self.x = self.col // QUAD, self.col % QUAD
         self.twin = self.chip * 2 + 1 - self.core
 
-    def on_core(self, k):
-        return ((self.chip + k) % HALF) * 2 + self.core
+    def on_core(self, k, other=0):
+        core = 1 - self.core if other else self.core
+        return (((self.low + k // QUAD) % 2) * QUAD + (self.y + near(k % QUAD)) % QUAD) * 2 + core
 
     def along_z(self, k):
         return ((self.z + k) % QUAD) * QUAD + self.x
@@ -130,73 +125,76 @@
         return self.z * QUAD + (self.x + k) % QUAD
 
 
+def near(k):
+    return k + k // 2 - 2 * (k // 3)
+
+
+def far(k):
+    return 2 - k + 3 * (k // 2) - 2 * (k // 3)
+
+
 def row_send(me, own, buf, send, recv):
     def one(k):
-        remote(own, buf.at[me.row], send, recv.at[me.row], me.on_core(k + 1), me.col).start()
+        remote(own, buf.at[me.row], send, recv.at[me.row], me.on_core(HALF - 1 - k), me.col).start()
 
     loop(HALF - 1, one)
     remote(own, buf.at[me.row], send, recv.at[me.row], me.twin, me.col).start()
 
 
-def row_relay(me, buf, send, recv, then=None):
-    def one(k):
-        slot = me.on_core(HALF - 1 - k)
+def row_relay(me, buf, send, recv):
+    def one(k):
+        slot = me.on_core(k + 1)
         wait_for(buf.at[slot], recv.at[slot])
         remote(buf.at[slot], buf.at[slot], send, recv.at[slot], me.twin, me.col).start()
-        if then:
-            then(slot)
 
     loop(HALF - 1, one)
 
 
-def row_finish(me, buf, recv, then=None):
-    def one(k):
-        slot = ((me.chip + HALF - k) % HALF) * 2 + 1 - me.core
+def row_finish(me, buf, recv, then):
+    def one(k):
+        then(me.on_core(k))
+        slot = me.on_core(k, other=1)
         wait_for(buf.at[slot], recv.at[slot])
-        if then:
-            then(slot)
+        then(slot)
 
     loop(HALF, one)
 
 
 def col_send(me, own, buf, send, recv):
-    def one(k):
-        remote(own, buf.at[me.col], send, recv.at[me.col], me.row, me.along_z(k + 1)).start()
+    def along_z(k):
+        remote(own, buf.at[me.col], send, recv.at[me.col], me.row, me.along_z(far(k))).start()
+
+    def along_x(k):
+        remote(own, buf.at[me.col], send, recv.at[me.col], me.row, me.along_x(far(k))).start()
+
+    loop(QUAD - 1, along_z)
+    loop(QUAD - 1, along_x)
+
+
+def col_relay(me, buf, send, recv):
+    def one(k):
+        slot = me.along_z(near(k + 1))
+        wait_for(buf.at[slot], recv.at[slot])
+
+        def two(q):
+            remote(buf.at[slot], buf.at[slot], send, recv.at[slot], me.row, me.along_x(far(q))).start()
+
+        loop(QUAD - 1, two)
 
     loop(QUAD - 1, one)
 
-    def two(k):
-        remote(own, buf.at[me.col], send, recv.at[me.col], me.row, me.along_x(k + 1)).start()
-
-    loop(QUAD - 1, two)
-
-
-def col_relay(me, buf, send, recv, then=None):
-    def one(k):
-        slot = me.along_z(QUAD - 1 - k)
+
+def col_finish(me, buf, recv, k, then):
+    group = (me.z + k) % QUAD
+    then(group * QUAD + me.x)
+
+    def one(q):
+        slot = group * QUAD + (me.x + near(q + 1)) % QUAD
         wait_for(buf.at[slot], recv.at[slot])
-
-        def two(q):
-            remote(buf.at[slot], buf.at[slot], send, recv.at[slot], me.row, me.along_x(q + 1)).start()
-
-        loop(QUAD - 1, two)
-        if then:
-            then(slot)
+        then(slot)
 
     loop(QUAD - 1, one)
-
-
-def col_finish(me, buf, recv, then=None):
-    def one(k):
-        def two(q):
-            slot = ((me.z + QUAD - k) % QUAD) * QUAD + (me.x + q + 1) % QUAD
-            wait_for(buf.at[slot], recv.at[slot])
-            if then:
-                then(slot)
-
-        loop(QUAD - 1, two)
-
-    loop(QUAD, one)
+    return group
 
 
 def stat_send(me, stat, buf, send, recv):
@@ -219,14 +217,14 @@
 
 def product_send(me, scaled, kernel, part, arrived, send, recv):
     def zs(k):
-        z = (me.z + k + 1) % QUAD
+        z = (me.z + far(k)) % QUAD
         rows = kernel[span(z, QUAD * W), :]
         product = lax.dot_general(scaled[...], rows, (((1,), (1,)), ((), ())), preferred_element_type=F32)
         for x in range(QUAD):
             part[z, x] = product[:, x * W : (x + 1) * W]
 
         def away(q):
-            x = (me.x + q + 1) % QUAD
+            x = (me.x + far(q)) % QUAD
             remote(part.at[z, x], arrived.at[z, me.x], send, recv.at[z], me.row, me.z * QUAD + x).start()
 
         loop(QUAD - 1, away)
@@ -235,14 +233,14 @@
     loop(QUAD, zs)
 
 
-def sum_send(me, arrived, sums, final, send, recv_x, recv_z, first, count):
-    def one(k):
-        z = (me.z + first + k + 1) % QUAD
+def sum_send(me, arrived, sums, final, send, recv_x, recv_z):
+    def one(k):
+        z = (me.z + far(k)) % QUAD
         wait_for(arrived.at[z, pl.ds(0, QUAD - 1)], recv_x.at[z])
         sums[z] = arrived[z, 0] + arrived[z, 1] + arrived[z, 2] + arrived[z, 3]
         remote(sums.at[z], final.at[me.z], send, recv_z, me.row, z * QUAD + me.x).start()
 
-    loop(count, one)
+    loop(QUAD - 1, one)
 
 
 def sum_own(me, arrived, final, recv_x):
@@ -259,12 +257,13 @@
     now_ref, next_ref, last_ref, pay_next_ref, pay_last_ref, out_next, out_now,
     x1, y1, x2, y2, v1, v2, own_v, pay_next, pay_last,
     earlier1, later1, earlier2, later2, log1, log2, kern, scaled,
-    peaks1, dens1, peaks2, dens2, peak, density1, density2, stat,
+    peaks1, dens1, peaks2, dens2, peak, density1, density2, stat, top,
     part1, arrived1, sums1, final1, part2, arrived2, sums2, final2,
     own_sem, gather_send, stat_sent, sum_sent_x, sum_sent_z,
     recv_gather, recv_stat, recv_x, recv_z,
 ):
     me = Place()
+    points, width = log1.shape[1], stat.shape[2]
 
     barrier = pltpu.get_barrier_semaphore()
 
@@ -298,10 +297,7 @@
         copy.wait()
     own_v[0] = pay_last[...].astype(F32)
     v1[me.row] = own_v[0]
-    build_earlier(x1, earlier1, me.col)
-    build_later(y1, later1, me.row)
-    build_earlier(x2, earlier2, me.col)
-    build_later(y2, later2, me.row)
+    top[...] = jnp.full_like(top, -jnp.inf)
     pl.semaphore_wait(barrier, SIDE - 1 + 2 * (QUAD - 1))
 
     g = lambda k: (gather_send.at[k], recv_gather.at[k])
@@ -312,46 +308,64 @@
 
     col_send(me, x1.at[me.col], x1, *g(0))
     row_send(me, y1.at[me.row], y1, *g(1))
-    row_relay(me, y1, *g(1), add_y1)
-    col_relay(me, x1, *g(0), add_x1)
+    row_relay(me, y1, *g(1))
+    col_relay(me, x1, *g(0))
     row_send(me, own_v.at[0], v1, *g(4))
     row_send(me, y2.at[me.row], y2, *g(3))
     col_send(me, x2.at[me.col], x2, *g(2))
     row_finish(me, y1, recv_gather.at[1], add_y1)
-    col_finish(me, x1, recv_gather.at[0], add_x1)
-
-    log_pass(earlier1, later1, log1, stat.at[0], 0)
-    stat_send(me, stat.at[0], peaks1.at[0], stat_sent.at[0, 0], recv_stat.at[0, 0])
+
+    def group_in(k):
+        group = col_finish(me, x1, recv_gather.at[0], near(k), add_x1)
+        log_tiles(earlier1, later1, log1, top, group * QUAD * W, QUAD * W, 0, points)
+
+    def stat_out(k, buf, half):
+        stat_send(me, stat.at[half], buf.at[half], stat_sent.at[k, half], recv_stat.at[k, half])
+
+    def peaks_out(half):
+        log_tiles(earlier1, later1, log1, top, last * QUAD * W, QUAD * W, half * width, width)
+        stat[half] = jnp.max(top[:, span(half, width)], axis=0, keepdims=True)
+        stat_out(0, peaks1, half)
+
+    loop(QUAD - 1, group_in)
+    last = col_finish(me, x1, recv_gather.at[0], 2, add_x1)
+    loop(HALVES, peaks_out)
+    top[...] = jnp.full_like(top, -jnp.inf)
+
     row_relay(me, v1, *g(4))
-    row_relay(me, y2, *g(3), add_y2)
-    log_pass(earlier1, later1, log1, stat.at[0], 1)
-    stat_send(me, stat.at[0], peaks1.at[1], stat_sent.at[0, 1], recv_stat.at[0, 1])
-    col_relay(me, x2, *g(2), add_x2)
+    row_relay(me, y2, *g(3))
+    col_relay(me, x2, *g(2))
     row_finish(me, y2, recv_gather.at[3], add_y2)
 
-    for half in range(HALVES):
+    def dens_out(half):
         stat_finish(peaks1.at[half], recv_stat.at[0, half], peak, half, jnp.maximum)
-        exp_pass(log1, kern, peak, stat.at[0], half)
-        stat_send(me, stat.at[0], dens1.at[half], stat_sent.at[1, half], recv_stat.at[1, half])
-
-    col_finish(me, x2, recv_gather.at[2], add_x2)
-    row_finish(me, v1, recv_gather.at[4])
-    for half in range(HALVES):
-        log_pass(earlier2, later2, log2, stat.at[0], half)
-        stat_send(me, stat.at[0], peaks2.at[half], stat_sent.at[2, half], recv_stat.at[2, half])
-
-    for half in range(HALVES):
-        stat_finish(dens1.at[half], recv_stat.at[1, half], density1, half, jnp.add)
+        exp_pass(log1, kern, peak, stat.at[half], half)
+        stat_out(1, dens1, half)
+
+    loop(HALVES, dens_out)
+
+    loop(QUAD, lambda k: (col_finish(me, x2, recv_gather.at[2], near(k), add_x2), None)[1])
+    row_finish(me, v1, recv_gather.at[4], lambda k: None)
+
+    def peaks_out_2(half):
+        part = width // 2
+        loop(2, lambda k: log_tiles(earlier2, later2, log2, top, 0, points, half * width + k * part, part))
+        stat[half] = jnp.max(top[:, span(half, width)], axis=0, keepdims=True)
+        stat_out(2, peaks2, half)
+
+    loop(HALVES, peaks_out_2)
+    loop(HALVES, lambda half: stat_finish(dens1.at[half], recv_stat.at[1, half], density1, half, jnp.add))
     scale(v1, density1, scaled)
     product_send(me, scaled, kern, part1, arrived1, sum_sent_x.at[0], recv_x.at[0])
 
-    sums = (arrived1, sums1, final1, sum_sent_z.at[0], recv_x.at[0], recv_z.at[0])
-    for half in range(HALVES):
+    def dens_out_2(half):
         stat_finish(peaks2.at[half], recv_stat.at[2, half], peak, half, jnp.maximum)
-        exp_pass(log2, kern, peak, stat.at[0], half)
-        stat_send(me, stat.at[0], dens2.at[half], stat_sent.at[3, half], recv_stat.at[3, half])
-        if half == 0:
-            sum_send(me, *sums, 0, QUAD - 1)
+        exp_pass(log2, kern, peak, stat.at[half], half)
+        stat_out(3, dens2, half)
+
+    dens_out_2(0)
+    sum_send(me, arrived1, sums1, final1, sum_sent_z.at[0], recv_x.at[0], recv_z.at[0])
+    dens_out_2(1)
     sum_own(me, arrived1, final1, recv_x.at[0])
     held = sum_finish(final1, recv_z.at[0])
     out_next[...] = held
@@ -360,13 +374,12 @@
     v2[me.row] = value_next
     row_send(me, own_v.at[1], v2, *g(5))
 
-    for half in range(HALVES):
-        stat_finish(dens2.at[half], recv_stat.at[3, half], density2, half, jnp.add)
+    loop(HALVES, lambda half: stat_finish(dens2.at[half], recv_stat.at[3, half], density2, half, jnp.add))
     row_relay(me, v2, *g(5))
-    row_finish(me, v2, recv_gather.at[5])
+    row_finish(me, v2, recv_gather.at[5], lambda k: None)
     scale(v2, density2, scaled)
     product_send(me, scaled, kern, part2, arrived2, sum_sent_x.at[1], recv_x.at[1])
-    sum_send(me, arrived2, sums2, final2, sum_sent_z.at[1], recv_x.at[1], recv_z.at[1], 0, QUAD - 1)
+    sum_send(me, arrived2, sums2, final2, sum_sent_z.at[1], recv_x.at[1], recv_z.at[1])
     sum_own(me, arrived2, final2, recv_x.at[1])
     out_now[...] = sum_finish(final2, recv_z.at[1])
 
@@ -406,6 +419,7 @@
         + [pltpu.VMEM((points, points), BF16), pltpu.VMEM((swaps, points), BF16)]
         + [stats] * 4
         + [line] * 4
+        + [pltpu.VMEM((8, points), F32)]
         + [square, square, quad, quad] * 2
         + [dma((6,)), dma((6,)), dma((4, HALVES)), dma((2,)), dma((2,))]
         + [dma((6, SIDE)), dma((4, HALVES)), dma((2, QUAD)), dma((2,))],

time: 73.3 us -> 70.1 us (0.956)
  Pallas kernels: 71 us -> 67.8 us
    pallas_call x1, Pallas kernels: 71 us -> 67.8 us  [per_device(): pl.pallas_call(kernel_body, out_shape=(out, out), in_specs=[pl.BlockSpec(...]
where the time goes in v3:
time: 70.1 us; the launch traced here: 69.9 us
  Pallas kernels  67.8 us (97%)
  other arithmetic  1.41 us (2%)
    pallas_call x1, Pallas kernels, per_device(): pl.pallas_call(kernel_body, out_shape=(out, out), in_specs=[pl.BlockSpec(...  67.8 us
    max x1, other arithmetic, per_device(): jnp.maximum(payoff_now.astype(F32), held_now)  1.41 us

profile of v3, /device:TPU:1, one launch (start us, length us, event | category | flops | bytes accessed | tf_op | source)
XLA Modules:
  0.0 69.9 jit_solution(13103258468283853032)
XLA Ops:
  0.6 0.0 copy-start
  0.6 0.0 copy-start.1
  0.7 67.8 %shard_map.77 = (f32[64,128]{1,0:T(8,128)}, f32[64,128]{1,0:T(8,128)}) custom-call(f32[40,128]{1,0:T(8,128)} %now_ref.1, f32[40,128]{1,0:T(8,128)} %next_ref.1, f32[40,128]{1,0:T(8,128)} %last_ref.1, bf16[64,128]{1,0:T(8,128)(2,1)} %pay_next_ref.1, bf16[64,128]{1,0:T(8,128)(2,1)} %pay_last_ref.1), custom_call_target="tpu_custom_call" | custom-call | tf_op jit(solution)/shard_map/pallas_call | solution.py:410
  68.5 0.0 copy-done
  68.5 0.0 copy-done.1
  68.5 1.4 %convert_maximum_fusion = (f32[64,128]{1,0:T(8,128)}, f32[64,128]{1,0:T(8,128)}) fusion(f32[64,128]{1,0:T(8,128)} %get-tuple-element.5, bf16[64,128]{1,0:T(8,128)(2,1)S(1)} %copy-done.1, f32[64,128]{1,0:T(8,128)} %get-tuple-element.4, bf16[64,128]{1,0:T(8,128)(2,1)S(1)} %copy-done), kind=kLoop, calls=%fused_computation | loop fusion | flops 32768 | bytes 163840 | tf_op jit(solution)/shard_map/max | solution.py:430
Async XLA Ops:
  0.6 67.9 %copy-start = (bf16[64,128]{1,0:T(8,128)(2,1)S(1)}, bf16[64,128]{1,0:T(8,128)(2,1)}, u32[]{:S(2)}) copy-start(bf16[64,128]{1,0:T(8,128)(2,1)} %pay_next_ref.1) | copy-start | bytes 49156
  0.6 67.9 %copy-start.1 = (bf16[64,128]{1,0:T(8,128)(2,1)S(1)}, bf16[64,128]{1,0:T(8,128)(2,1)}, u32[]{:S(2)}) copy-start(bf16[64,128]{1,0:T(8,128)(2,1)} %param.9) | copy-start | bytes 49156

commit v4 on v3

--- a/solution.py
+++ b/solution.py
@@ -353,7 +353,7 @@
         stat[half] = jnp.max(top[:, span(half, width)], axis=0, keepdims=True)
         stat_out(2, peaks2, half)
 
-    loop(HALVES, peaks_out_2)
+    peaks_out_2(0)
     loop(HALVES, lambda half: stat_finish(dens1.at[half], recv_stat.at[1, half], density1, half, jnp.add))
     scale(v1, density1, scaled)
     product_send(me, scaled, kern, part1, arrived1, sum_sent_x.at[0], recv_x.at[0])
@@ -363,9 +363,9 @@
         exp_pass(log2, kern, peak, stat.at[half], half)
         stat_out(3, dens2, half)
 
-    dens_out_2(0)
+    peaks_out_2(1)
     sum_send(me, arrived1, sums1, final1, sum_sent_z.at[0], recv_x.at[0], recv_z.at[0])
-    dens_out_2(1)
+    loop(HALVES, dens_out_2)
     sum_own(me, arrived1, final1, recv_x.at[0])
     held = sum_finish(final1, recv_z.at[0])
     out_next[...] = held

time: 70.1 us -> 68.3 us (0.974)
  Pallas kernels: 67.8 us -> 66 us
    pallas_call x1, Pallas kernels: 67.8 us -> 66 us  [per_device(): pl.pallas_call(kernel_body, out_shape=(out, out), in_specs=[pl.BlockSpec(...]
where the time goes in v4:
time: 68.3 us; the launch traced here: 68.1 us
  Pallas kernels  66 us (97%)
  other arithmetic  1.41 us (2%)
    pallas_call x1, Pallas kernels, per_device(): pl.pallas_call(kernel_body, out_shape=(out, out), in_specs=[pl.BlockSpec(...  66 us
    max x1, other arithmetic, per_device(): jnp.maximum(payoff_now.astype(F32), held_now)  1.41 us

profile of v4, /device:TPU:1, one launch (start us, length us, event | category | flops | bytes accessed | tf_op | source)
XLA Modules:
  0.0 68.1 jit_solution(9479000472299096602)
XLA Ops:
  0.6 0.0 copy-start
  0.6 0.0 copy-start.1
  0.7 66.0 %shard_map.77 = (f32[64,128]{1,0:T(8,128)}, f32[64,128]{1,0:T(8,128)}) custom-call(f32[40,128]{1,0:T(8,128)} %now_ref.1, f32[40,128]{1,0:T(8,128)} %next_ref.1, f32[40,128]{1,0:T(8,128)} %last_ref.1, bf16[64,128]{1,0:T(8,128)(2,1)} %pay_next_ref.1, bf16[64,128]{1,0:T(8,128)(2,1)} %pay_last_ref.1), custom_call_target="tpu_custom_call" | custom-call | tf_op jit(solution)/shard_map/pallas_call | solution.py:410
  66.7 0.0 copy-done
  66.7 0.0 copy-done.1
  66.7 1.4 %convert_maximum_fusion = (f32[64,128]{1,0:T(8,128)}, f32[64,128]{1,0:T(8,128)}) fusion(f32[64,128]{1,0:T(8,128)} %get-tuple-element.5, bf16[64,128]{1,0:T(8,128)(2,1)S(1)} %copy-done.1, f32[64,128]{1,0:T(8,128)} %get-tuple-element.4, bf16[64,128]{1,0:T(8,128)(2,1)S(1)} %copy-done), kind=kLoop, calls=%fused_computation | loop fusion | flops 32768 | bytes 163840 | tf_op jit(solution)/shard_map/max | solution.py:430
Async XLA Ops:
  0.6 66.1 %copy-start = (bf16[64,128]{1,0:T(8,128)(2,1)S(1)}, bf16[64,128]{1,0:T(8,128)(2,1)}, u32[]{:S(2)}) copy-start(bf16[64,128]{1,0:T(8,128)(2,1)} %pay_next_ref.1) | copy-start | bytes 49156
  0.6 66.1 %copy-start.1 = (bf16[64,128]{1,0:T(8,128)(2,1)S(1)}, bf16[64,128]{1,0:T(8,128)(2,1)}, u32[]{:S(2)}) copy-start(bf16[64,128]{1,0:T(8,128)(2,1)} %param.9) | copy-start | bytes 49156

commit v5 on v4

--- a/solution.py
+++ b/solution.py
@@ -65,35 +65,51 @@
         top[:, js] = highest
 
 
-def exp_pass(log_kernel, kernel, peak, stat, half):
+def exp_pass(log_kernel, top, stat, half):
     rows, cols = 64, 256
     blocks = log_kernel.shape[1] // cols // HALVES
 
     def col(jc):
         js = span(half * blocks + jc, cols)
-        top = jnp.broadcast_to(peak[half, :, span(jc, cols)], (8, cols))
+        peak = jnp.max(top[:, js], axis=0, keepdims=True)
+        stat[0, :, span(jc, cols)] = peak
+        peak = jnp.broadcast_to(peak, (8, cols))
 
         def row(ic, total):
             i = span(ic, rows)
-            tile = jnp.exp(log_kernel[i, js].reshape(rows // 8, 8, cols) - top[None])
-            kernel[i, js] = tile.reshape(rows, cols).astype(BF16)
+            tile = jnp.exp(log_kernel[i, js].reshape(rows // 8, 8, cols) - peak[None])
+            log_kernel[i, js] = tile.reshape(rows, cols)
             return total + jnp.sum(tile, axis=0)
 
         count = log_kernel.shape[0] // rows
         total = lax.fori_loop(0, count, row, jnp.zeros((8, cols), F32), unroll=True)
-        stat[:, span(jc, cols)] = jnp.sum(total, axis=0, keepdims=True)
+        stat[1, :, span(jc, cols)] = jnp.sum(total, axis=0, keepdims=True)
 
     loop(blocks, col)
 
 
+def kernel_tile(weights, factor, kernel, group):
+    rows, cols = QUAD * W, 512
+    blocks = kernel.shape[1] // cols
+
+    def col(jc):
+        part = blocks // HALVES
+        own = jnp.broadcast_to(factor[jc // part, :, span(jc % part, cols)], (8, cols))
+        js = span(jc, cols)
+        piece = weights[span(group, rows), js].reshape(rows // 8, 8, cols) * own[None]
+        kernel[span(group, rows), js] = piece.reshape(rows, cols).astype(BF16)
+
+    loop(blocks, col)
+
+
 def scale(values, density, scaled):
+    loop(SIDE, lambda k: scale_block(values, density, scaled, k))
+
+
+def scale_block(values, density, scaled, k):
     blocks = SIDE // HALVES
-
-    def one(k):
-        below = density[k // blocks, :, span(k % blocks, W)]
-        scaled[:, span(k, W)] = (values[k] / below).astype(BF16)
-
-    loop(SIDE, one)
+    below = density[k // blocks, :, span(k % blocks, W)]
+    scaled[:, span(k, W)] = (values[k] / below).astype(BF16)
 
 
 def remote(src, dst, send, recv, row, col):
@@ -207,19 +223,24 @@
     loop(SIDE - 1, one)
 
 
-def stat_finish(buf, recv, out, half, combine):
+def stat_finish(me, buf, recv, factor, density, half):
     wait_for(buf.at[pl.ds(0, SIDE - 1)], recv)
-    total = buf[0]
+    peak = buf[0, 0]
     for k in range(1, SIDE):
-        total = combine(total, buf[k])
-    out[half] = total
-
-
-def product_send(me, scaled, kernel, part, arrived, send, recv):
+        peak = jnp.maximum(peak, buf[k, 0])
+    total = buf[0, 1] * jnp.exp(buf[0, 0] - peak)
+    for k in range(1, SIDE):
+        total = total + buf[k, 1] * jnp.exp(buf[k, 0] - peak)
+    density[half] = total
+    factor[half] = jnp.exp(buf[me.row, 0] - peak)
+
+
+def product_send(me, scaled, kernel, form, part, arrived, send, recv):
     def zs(k):
         z = (me.z + far(k)) % QUAD
-        rows = kernel[span(z, QUAD * W), :]
-        product = lax.dot_general(scaled[...], rows, (((1,), (1,)), ((), ())), preferred_element_type=F32)
+        if form:
+            form(z)
+        product = lax.dot_general(scaled[...], kernel[span(z, QUAD * W), :], (((1,), (1,)), ((), ())), preferred_element_type=F32)
         for x in range(QUAD):
             part[z, x] = product[:, x * W : (x + 1) * W]
 
@@ -257,13 +278,13 @@
     now_ref, next_ref, last_ref, pay_next_ref, pay_last_ref, out_next, out_now,
     x1, y1, x2, y2, v1, v2, own_v, pay_next, pay_last,
     earlier1, later1, earlier2, later2, log1, log2, kern, scaled,
-    peaks1, dens1, peaks2, dens2, peak, density1, density2, stat, top,
+    stats1, stats2, factor1, factor2, density1, density2, stat, top,
     part1, arrived1, sums1, final1, part2, arrived2, sums2, final2,
     own_sem, gather_send, stat_sent, sum_sent_x, sum_sent_z,
     recv_gather, recv_stat, recv_x, recv_z,
 ):
     me = Place()
-    points, width = log1.shape[1], stat.shape[2]
+    points, width = log1.shape[1], stat.shape[3]
 
     barrier = pltpu.get_barrier_semaphore()
 
@@ -322,14 +343,14 @@
     def stat_out(k, buf, half):
         stat_send(me, stat.at[half], buf.at[half], stat_sent.at[k, half], recv_stat.at[k, half])
 
-    def peaks_out(half):
+    def stats_out(half):
         log_tiles(earlier1, later1, log1, top, last * QUAD * W, QUAD * W, half * width, width)
-        stat[half] = jnp.max(top[:, span(half, width)], axis=0, keepdims=True)
-        stat_out(0, peaks1, half)
+        exp_pass(log1, top, stat.at[half], half)
+        stat_out(0, stats1, half)
 
     loop(QUAD - 1, group_in)
     last = col_finish(me, x1, recv_gather.at[0], 2, add_x1)
-    loop(HALVES, peaks_out)
+    loop(HALVES, stats_out)
     top[...] = jnp.full_like(top, -jnp.inf)
 
     row_relay(me, v1, *g(4))
@@ -337,35 +358,24 @@
     col_relay(me, x2, *g(2))
     row_finish(me, y2, recv_gather.at[3], add_y2)
 
-    def dens_out(half):
-        stat_finish(peaks1.at[half], recv_stat.at[0, half], peak, half, jnp.maximum)
-        exp_pass(log1, kern, peak, stat.at[half], half)
-        stat_out(1, dens1, half)
-
-    loop(HALVES, dens_out)
-
     loop(QUAD, lambda k: (col_finish(me, x2, recv_gather.at[2], near(k), add_x2), None)[1])
     row_finish(me, v1, recv_gather.at[4], lambda k: None)
 
-    def peaks_out_2(half):
+    def log_2(half):
         part = width // 2
         loop(2, lambda k: log_tiles(earlier2, later2, log2, top, 0, points, half * width + k * part, part))
-        stat[half] = jnp.max(top[:, span(half, width)], axis=0, keepdims=True)
-        stat_out(2, peaks2, half)
-
-    peaks_out_2(0)
-    loop(HALVES, lambda half: stat_finish(dens1.at[half], recv_stat.at[1, half], density1, half, jnp.add))
+
+    def stats_out_2(half):
+        exp_pass(log2, top, stat.at[half], half)
+        stat_out(1, stats2, half)
+
+    log_2(0)
+    loop(HALVES, lambda half: stat_finish(me, stats1.at[half], recv_stat.at[0, half], factor1, density1, half))
     scale(v1, density1, scaled)
-    product_send(me, scaled, kern, part1, arrived1, sum_sent_x.at[0], recv_x.at[0])
-
-    def dens_out_2(half):
-        stat_finish(peaks2.at[half], recv_stat.at[2, half], peak, half, jnp.maximum)
-        exp_pass(log2, kern, peak, stat.at[half], half)
-        stat_out(3, dens2, half)
-
-    peaks_out_2(1)
+    product_send(me, scaled, kern, lambda z: kernel_tile(log1, factor1, kern, z), part1, arrived1, sum_sent_x.at[0], recv_x.at[0])
+    log_2(1)
     sum_send(me, arrived1, sums1, final1, sum_sent_z.at[0], recv_x.at[0], recv_z.at[0])
-    loop(HALVES, dens_out_2)
+    loop(HALVES, stats_out_2)
     sum_own(me, arrived1, final1, recv_x.at[0])
     held = sum_finish(final1, recv_z.at[0])
     out_next[...] = held
@@ -374,18 +384,18 @@
     v2[me.row] = value_next
     row_send(me, own_v.at[1], v2, *g(5))
 
-    loop(HALVES, lambda half: stat_finish(dens2.at[half], recv_stat.at[3, half], density2, half, jnp.add))
+    loop(HALVES, lambda half: stat_finish(me, stats2.at[half], recv_stat.at[1, half], factor2, density2, half))
     row_relay(me, v2, *g(5))
-    row_finish(me, v2, recv_gather.at[5], lambda k: None)
-    scale(v2, density2, scaled)
-    product_send(me, scaled, kern, part2, arrived2, sum_sent_x.at[1], recv_x.at[1])
+    loop(QUAD, lambda z: kernel_tile(log2, factor2, kern, z))
+    row_finish(me, v2, recv_gather.at[5], lambda k: scale_block(v2, density2, scaled, k))
+    product_send(me, scaled, kern, None, part2, arrived2, sum_sent_x.at[1], recv_x.at[1])
     sum_send(me, arrived2, sums2, final2, sum_sent_z.at[1], recv_x.at[1], recv_z.at[1])
     sum_own(me, arrived2, final2, recv_x.at[1])
     out_now[...] = sum_finish(final2, recv_z.at[1])
 
     for k, buf in ((0, x1), (1, y1), (2, x2), (3, y2), (4, v1), (5, v2)):
         wait_for(buf.at[pl.ds(0, SIDE - 1)], gather_send.at[k])
-    for k, buf in ((0, peaks1), (1, dens1), (2, peaks2), (3, dens2)):
+    for k, buf in ((0, stats1), (1, stats2)):
         for half in range(HALVES):
             wait_for(buf.at[half, pl.ds(0, SIDE - 1)], stat_sent.at[k, half])
     for k, part, final in ((0, part1, final1), (1, part2, final2)):
@@ -399,7 +409,7 @@
     points = SIDE * width
     states = pltpu.VMEM((SIDE, factors, width), F32)
     values = pltpu.VMEM((SIDE, swaps, width), F32)
-    stats = pltpu.VMEM((HALVES, SIDE, 1, points // HALVES), F32)
+    stats = pltpu.VMEM((HALVES, SIDE, 2, 1, points // HALVES), F32)
     line = pltpu.VMEM((HALVES, 1, points // HALVES), F32)
     quad = pltpu.VMEM((QUAD, swaps, width), F32)
     square = pltpu.VMEM((QUAD, QUAD, swaps, width), F32)
@@ -417,12 +427,13 @@
         + [pltpu.VMEM((points, 256), BF16), pltpu.VMEM((256, points), BF16)] * 2
         + [pltpu.VMEM((points, points), F32)] * 2
         + [pltpu.VMEM((points, points), BF16), pltpu.VMEM((swaps, points), BF16)]
-        + [stats] * 4
+        + [stats] * 2
         + [line] * 4
+        + [pltpu.VMEM((HALVES, 2, 1, points // HALVES), F32)]
         + [pltpu.VMEM((8, points), F32)]
         + [square, square, quad, quad] * 2
-        + [dma((6,)), dma((6,)), dma((4, HALVES)), dma((2,)), dma((2,))]
-        + [dma((6, SIDE)), dma((4, HALVES)), dma((2, QUAD)), dma((2,))],
+        + [dma((6,)), dma((6,)), dma((2, HALVES)), dma((2,)), dma((2,))]
+        + [dma((6, SIDE)), dma((2, HALVES)), dma((2, QUAD)), dma((2,))],
         compiler_params=pltpu.CompilerParams(
             collective_id=0, has_side_effects=True, vmem_limit_bytes=60 * 2**20
         ),

time: 68.3 us -> 66.3 us (0.971)
  Pallas kernels: 66 us -> 64 us
    pallas_call x1, Pallas kernels: 66 us -> 64 us  [per_device(): pl.pallas_call(kernel_body, out_shape=(out, out), in_specs=[pl.BlockSpec(...]
where the time goes in v5:
time: 66.3 us; the launch traced here: 66.1 us
  Pallas kernels  64 us (97%)
  other arithmetic  1.41 us (2%)
  between operations  0.67 us (1%)
    pallas_call x1, Pallas kernels, per_device(): pl.pallas_call(kernel_body, out_shape=(out, out), in_specs=[pl.BlockSpec(...  64 us
    max x1, other arithmetic, per_device(): jnp.maximum(payoff_now.astype(F32), held_now)  1.41 us

profile of v5, /device:TPU:1, one launch (start us, length us, event | category | flops | bytes accessed | tf_op | source)
XLA Modules:
  0.0 66.1 jit_solution(2332495083032831054)
XLA Ops:
  0.6 0.0 copy-start
  0.6 0.0 copy-start.1
  0.7 64.0 %shard_map.77 = (f32[64,128]{1,0:T(8,128)}, f32[64,128]{1,0:T(8,128)}) custom-call(f32[40,128]{1,0:T(8,128)} %now_ref.1, f32[40,128]{1,0:T(8,128)} %next_ref.1, f32[40,128]{1,0:T(8,128)} %last_ref.1, bf16[64,128]{1,0:T(8,128)(2,1)} %pay_next_ref.1, bf16[64,128]{1,0:T(8,128)(2,1)} %pay_last_ref.1), custom_call_target="tpu_custom_call" | custom-call | tf_op jit(solution)/shard_map/pallas_call | solution.py:420
  64.7 0.0 copy-done
  64.7 0.0 copy-done.1
  64.7 1.4 %convert_maximum_fusion = (f32[64,128]{1,0:T(8,128)}, f32[64,128]{1,0:T(8,128)}) fusion(f32[64,128]{1,0:T(8,128)} %get-tuple-element.5, bf16[64,128]{1,0:T(8,128)(2,1)S(1)} %copy-done.1, f32[64,128]{1,0:T(8,128)} %get-tuple-element.4, bf16[64,128]{1,0:T(8,128)(2,1)S(1)} %copy-done), kind=kLoop, calls=%fused_computation | loop fusion | flops 32768 | bytes 163840 | tf_op jit(solution)/shard_map/max | solution.py:441
Async XLA Ops:
  0.6 64.0 %copy-start = (bf16[64,128]{1,0:T(8,128)(2,1)S(1)}, bf16[64,128]{1,0:T(8,128)(2,1)}, u32[]{:S(2)}) copy-start(bf16[64,128]{1,0:T(8,128)(2,1)} %pay_next_ref.1) | copy-start | bytes 49156
  0.6 64.0 %copy-start.1 = (bf16[64,128]{1,0:T(8,128)(2,1)S(1)}, bf16[64,128]{1,0:T(8,128)(2,1)}, u32[]{:S(2)}) copy-start(bf16[64,128]{1,0:T(8,128)(2,1)} %param.9) | copy-start | bytes 49156

commit v6 on v5

--- a/solution.py
+++ b/solution.py
@@ -9,7 +9,7 @@
 W = 128
 SIDE = 16
 QUAD = 4
-HALVES = 2
+PARTS = 4
 HALF = 8
 MESH = pl.DeviceIdType.MESH
 
@@ -65,12 +65,12 @@
         top[:, js] = highest
 
 
-def exp_pass(log_kernel, top, stat, half):
+def exp_pass(log_kernel, top, stat, part_at):
     rows, cols = 64, 256
-    blocks = log_kernel.shape[1] // cols // HALVES
+    blocks = log_kernel.shape[1] // cols // PARTS
 
     def col(jc):
-        js = span(half * blocks + jc, cols)
+        js = span(part_at * blocks + jc, cols)
         peak = jnp.max(top[:, js], axis=0, keepdims=True)
         stat[0, :, span(jc, cols)] = peak
         peak = jnp.broadcast_to(peak, (8, cols))
@@ -93,7 +93,7 @@
     blocks = kernel.shape[1] // cols
 
     def col(jc):
-        part = blocks // HALVES
+        part = blocks // PARTS
         own = jnp.broadcast_to(factor[jc // part, :, span(jc % part, cols)], (8, cols))
         js = span(jc, cols)
         piece = weights[span(group, rows), js].reshape(rows // 8, 8, cols) * own[None]
@@ -107,7 +107,7 @@
 
 
 def scale_block(values, density, scaled, k):
-    blocks = SIDE // HALVES
+    blocks = SIDE // PARTS
     below = density[k // blocks, :, span(k % blocks, W)]
     scaled[:, span(k, W)] = (values[k] / below).astype(BF16)
 
@@ -223,7 +223,7 @@
     loop(SIDE - 1, one)
 
 
-def stat_finish(me, buf, recv, factor, density, half):
+def stat_finish(me, buf, recv, factor, density, part_at):
     wait_for(buf.at[pl.ds(0, SIDE - 1)], recv)
     peak = buf[0, 0]
     for k in range(1, SIDE):
@@ -231,8 +231,8 @@
     total = buf[0, 1] * jnp.exp(buf[0, 0] - peak)
     for k in range(1, SIDE):
         total = total + buf[k, 1] * jnp.exp(buf[k, 0] - peak)
-    density[half] = total
-    factor[half] = jnp.exp(buf[me.row, 0] - peak)
+    density[part_at] = total
+    factor[part_at] = jnp.exp(buf[me.row, 0] - peak)
 
 
 def product_send(me, scaled, kernel, form, part, arrived, send, recv):
@@ -340,17 +340,17 @@
         group = col_finish(me, x1, recv_gather.at[0], near(k), add_x1)
         log_tiles(earlier1, later1, log1, top, group * QUAD * W, QUAD * W, 0, points)
 
-    def stat_out(k, buf, half):
-        stat_send(me, stat.at[half], buf.at[half], stat_sent.at[k, half], recv_stat.at[k, half])
-
-    def stats_out(half):
-        log_tiles(earlier1, later1, log1, top, last * QUAD * W, QUAD * W, half * width, width)
-        exp_pass(log1, top, stat.at[half], half)
-        stat_out(0, stats1, half)
+    def stat_out(k, buf, part_at):
+        stat_send(me, stat.at[part_at], buf.at[part_at], stat_sent.at[k, part_at], recv_stat.at[k, part_at])
+
+    def stats_out(part_at):
+        log_tiles(earlier1, later1, log1, top, last * QUAD * W, QUAD * W, part_at * width, width)
+        exp_pass(log1, top, stat.at[part_at], part_at)
+        stat_out(0, stats1, part_at)
 
     loop(QUAD - 1, group_in)
     last = col_finish(me, x1, recv_gather.at[0], 2, add_x1)
-    loop(HALVES, stats_out)
+    loop(PARTS, stats_out)
     top[...] = jnp.full_like(top, -jnp.inf)
 
     row_relay(me, v1, *g(4))
@@ -361,21 +361,21 @@
     loop(QUAD, lambda k: (col_finish(me, x2, recv_gather.at[2], near(k), add_x2), None)[1])
     row_finish(me, v1, recv_gather.at[4], lambda k: None)
 
-    def log_2(half):
+    def log_2(part_at):
         part = width // 2
-        loop(2, lambda k: log_tiles(earlier2, later2, log2, top, 0, points, half * width + k * part, part))
-
-    def stats_out_2(half):
-        exp_pass(log2, top, stat.at[half], half)
-        stat_out(1, stats2, half)
-
-    log_2(0)
-    loop(HALVES, lambda half: stat_finish(me, stats1.at[half], recv_stat.at[0, half], factor1, density1, half))
+        loop(2, lambda k: log_tiles(earlier2, later2, log2, top, 0, points, part_at * width + k * part, part))
+
+    def stats_out_2(part_at):
+        exp_pass(log2, top, stat.at[part_at], part_at)
+        stat_out(1, stats2, part_at)
+
+    loop(PARTS // 2, log_2)
+    loop(PARTS, lambda part_at: stat_finish(me, stats1.at[part_at], recv_stat.at[0, part_at], factor1, density1, part_at))
     scale(v1, density1, scaled)
     product_send(me, scaled, kern, lambda z: kernel_tile(log1, factor1, kern, z), part1, arrived1, sum_sent_x.at[0], recv_x.at[0])
-    log_2(1)
+    loop(PARTS // 2, lambda part: log_2(PARTS // 2 + part))
     sum_send(me, arrived1, sums1, final1, sum_sent_z.at[0], recv_x.at[0], recv_z.at[0])
-    loop(HALVES, stats_out_2)
+    loop(PARTS, stats_out_2)
     sum_own(me, arrived1, final1, recv_x.at[0])
     held = sum_finish(final1, recv_z.at[0])
     out_next[...] = held
@@ -384,7 +384,7 @@
     v2[me.row] = value_next
     row_send(me, own_v.at[1], v2, *g(5))
 
-    loop(HALVES, lambda half: stat_finish(me, stats2.at[half], recv_stat.at[1, half], factor2, density2, half))
+    loop(PARTS, lambda part_at: stat_finish(me, stats2.at[part_at], recv_stat.at[1, part_at], factor2, density2, part_at))
     row_relay(me, v2, *g(5))
     loop(QUAD, lambda z: kernel_tile(log2, factor2, kern, z))
     row_finish(me, v2, recv_gather.at[5], lambda k: scale_block(v2, density2, scaled, k))
@@ -396,8 +396,8 @@
     for k, buf in ((0, x1), (1, y1), (2, x2), (3, y2), (4, v1), (5, v2)):
         wait_for(buf.at[pl.ds(0, SIDE - 1)], gather_send.at[k])
     for k, buf in ((0, stats1), (1, stats2)):
-        for half in range(HALVES):
-            wait_for(buf.at[half, pl.ds(0, SIDE - 1)], stat_sent.at[k, half])
+        for part_at in range(PARTS):
+            wait_for(buf.at[part_at, pl.ds(0, SIDE - 1)], stat_sent.at[k, part_at])
     for k, part, final in ((0, part1, final1), (1, part2, final2)):
         wait_for(part.at[pl.ds(0, QUAD - 1)], sum_sent_x.at[k])
         wait_for(final.at[pl.ds(0, QUAD - 1)], sum_sent_z.at[k])
@@ -409,8 +409,8 @@
     points = SIDE * width
     states = pltpu.VMEM((SIDE, factors, width), F32)
     values = pltpu.VMEM((SIDE, swaps, width), F32)
-    stats = pltpu.VMEM((HALVES, SIDE, 2, 1, points // HALVES), F32)
-    line = pltpu.VMEM((HALVES, 1, points // HALVES), F32)
+    stats = pltpu.VMEM((PARTS, SIDE, 2, 1, points // PARTS), F32)
+    line = pltpu.VMEM((PARTS, 1, points // PARTS), F32)
     quad = pltpu.VMEM((QUAD, swaps, width), F32)
     square = pltpu.VMEM((QUAD, QUAD, swaps, width), F32)
     payoff = pltpu.VMEM((swaps, width), BF16)
@@ -429,11 +429,11 @@
         + [pltpu.VMEM((points, points), BF16), pltpu.VMEM((swaps, points), BF16)]
         + [stats] * 2
         + [line] * 4
-        + [pltpu.VMEM((HALVES, 2, 1, points // HALVES), F32)]
+        + [pltpu.VMEM((PARTS, 2, 1, points // PARTS), F32)]
         + [pltpu.VMEM((8, points), F32)]
         + [square, square, quad, quad] * 2
-        + [dma((6,)), dma((6,)), dma((2, HALVES)), dma((2,)), dma((2,))]
-        + [dma((6, SIDE)), dma((2, HALVES)), dma((2, QUAD)), dma((2,))],
+        + [dma((6,)), dma((6,)), dma((2, PARTS)), dma((2,)), dma((2,))]
+        + [dma((6, SIDE)), dma((2, PARTS)), dma((2, QUAD)), dma((2,))],
         compiler_params=pltpu.CompilerParams(
             collective_id=0, has_side_effects=True, vmem_limit_bytes=60 * 2**20
         ),

time: 66.3 us -> 67.9 us (1.024)
  Pallas kernels: 64 us -> 65.5 us
    pallas_call x1, Pallas kernels: 64 us -> 65.5 us  [per_device(): pl.pallas_call(kernel_body, out_shape=(out, out), in_specs=[pl.BlockSpec(...]
where the time goes in v6:
time: 67.9 us; the launch traced here: 67.6 us
  Pallas kernels  65.5 us (96%)
  other arithmetic  1.41 us (2%)
    pallas_call x1, Pallas kernels, per_device(): pl.pallas_call(kernel_body, out_shape=(out, out), in_specs=[pl.BlockSpec(...  65.5 us
    max x1, other arithmetic, per_device(): jnp.maximum(payoff_now.astype(F32), held_now)  1.41 us

profile of v6, /device:TPU:1, one launch (start us, length us, event | category | flops | bytes accessed | tf_op | source)
XLA Modules:
  0.0 67.6 jit_solution(5054782636800219364)
XLA Ops:
  0.6 0.0 copy-start
  0.6 0.0 copy-start.1
  0.7 65.5 %shard_map.77 = (f32[64,128]{1,0:T(8,128)}, f32[64,128]{1,0:T(8,128)}) custom-call(f32[40,128]{1,0:T(8,128)} %now_ref.1, f32[40,128]{1,0:T(8,128)} %next_ref.1, f32[40,128]{1,0:T(8,128)} %last_ref.1, bf16[64,128]{1,0:T(8,128)(2,1)} %pay_next_ref.1, bf16[64,128]{1,0:T(8,128)(2,1)} %pay_last_ref.1), custom_call_target="tpu_custom_call" | custom-call | tf_op jit(solution)/shard_map/pallas_call | solution.py:420
  66.2 0.0 copy-done
  66.2 0.0 copy-done.1
  66.2 1.4 %convert_maximum_fusion = (f32[64,128]{1,0:T(8,128)}, f32[64,128]{1,0:T(8,128)}) fusion(f32[64,128]{1,0:T(8,128)} %get-tuple-element.5, bf16[64,128]{1,0:T(8,128)(2,1)S(1)} %copy-done.1, f32[64,128]{1,0:T(8,128)} %get-tuple-element.4, bf16[64,128]{1,0:T(8,128)(2,1)S(1)} %copy-done), kind=kLoop, calls=%fused_computation | loop fusion | flops 32768 | bytes 163840 | tf_op jit(solution)/shard_map/max | solution.py:441
Async XLA Ops:
  0.6 65.6 %copy-start = (bf16[64,128]{1,0:T(8,128)(2,1)S(1)}, bf16[64,128]{1,0:T(8,128)(2,1)}, u32[]{:S(2)}) copy-start(bf16[64,128]{1,0:T(8,128)(2,1)} %pay_next_ref.1) | copy-start | bytes 49156
  0.6 65.6 %copy-start.1 = (bf16[64,128]{1,0:T(8,128)(2,1)S(1)}, bf16[64,128]{1,0:T(8,128)(2,1)}, u32[]{:S(2)}) copy-start(bf16[64,128]{1,0:T(8,128)(2,1)} %param.9) | copy-start | bytes 49156
